TPU v7x, 512 devices: a whole 4x4x16 slice. The times are simulated.
512 devices in a mesh: gz: 64 (over y, z), xy: 8 (over x, core).
Axes of the slice: x: 4, y: 4, z: 16, core: 2. Of those that a mesh axis runs over, the one named last changes fastest.
Arguments:
- right_side: float32 [2, 64, 64, 2048], P(None, 'gz', 'xy')
- stiff_across: float32 [64, 64, 2048], P('gz', 'xy'), may hold values from 0.3 to 3
- stiff_down: float32 [64, 64, 2048], P('gz', 'xy'), may hold values from 0.3 to 3
- anchor: float32 [64, 64, 2048], P('gz', 'xy'), may hold values from 0.02 to 0.2
- source_node: int32 [64, 8, 1024], P('gz', 'xy'), may hold values from 0 to 16383
- target_cell: int32 [64, 8, 1024], P('gz', 'xy'), may hold values from 0 to 14334, as said below
- corner_weight: float32 [4, 64, 8, 1024], P(None, 'gz', 'xy'), may hold values from 0 to 1, as said below
- block_count: int32 [64, 8], P('gz', 'xy'), may hold values from 1 to 8, as said below
Outputs:
- solution_field: float32 [2, 64, 64, 2048], P(None, 'gz', 'xy')
- residual: float32 [2, 64, 64, 2048], P(None, 'gz', 'xy')
Inputs may be any that keep to these rules, and one draw needn't show every extreme that they name: `target_cell`: each target cell's row is below 7 and its column below 2047 within the block, so all four corners lie in the same block. `corner_weight`: the weights of a slot are nonnegative and sum to 1. `block_count`: some device holds exactly 8 used blocks.
All inputs are finite; a program needn't handle non-finite values.
Results may differ from a plain program's by a relative error of at most 0.00013.
Values sent between devices are 32-bit elements; how exact they have to be, the bound alone decides.
A program may use at most 64 MiB of HBM per device.

v0:
```python
import jax
import jax.numpy as jnp
from jax import lax
from jax.sharding import Mesh
from jax.sharding import PartitionSpec as P

BLOCK = 128
ITERS = 3
GZ_XY = ("gz_0", "gz_1", "xy_0", "xy_1")
GZ = ("gz_0", "gz_1")
XY = ("xy_0", "xy_1")


def one_axis_at_a_time(shard, axes):
    for axis in axes:
        shard = lax.psum(shard, axis)
    return shard


def passed_along(block, axis, distance):
    devices = range(lax.axis_size(axis))
    route = [(i - distance, i) for i in devices if i - distance in devices]
    return lax.ppermute(block, axis, route)


def padded_2(cells, sides, width):
    for axis, dim in sides:
        count = lax.axis_size(axis)
        ends = count - 1
        head = lax.slice_in_dim(cells, 0, width, axis=dim)
        tail = lax.slice_in_dim(cells, cells.shape[dim] - width, cells.shape[dim], axis=dim)
        cells = jnp.concatenate(
            [
                lax.ppermute(tail, axis, [(i, (i + 1) % count) for i in range(ends)]),
                cells,
                lax.ppermute(head, axis, [((i + 1) % count, i) for i in range(ends)]),
            ],
            axis=dim,
        )
    return cells


def two_products(residual, image):
    return (
        one_axis_at_a_time(jnp.sum(residual * residual), GZ_XY),
        one_axis_at_a_time(jnp.sum(residual * image), GZ_XY),
    )


def body(
    right_side,
    stiff_across,
    stiff_down,
    anchor,
    source_node,
    target_cell,
    corner_weight,
    block_count,
):
    rows = stiff_across.shape[1]
    cols = stiff_across.shape[2]
    rhs = right_side[:, 0]
    across = stiff_across[0]
    down = stiff_down[0]
    hold = anchor[0]
    source = source_node[0, 0]
    target = target_cell[0, 0]
    weights = corner_weight[:, 0, 0]
    count = block_count[0, 0]
    slots = source.shape[0]
    has_next = lax.axis_index(GZ) < lax.axis_size(GZ) - 1
    live = ((jnp.arange(slots, dtype=jnp.int32) < count * BLOCK) & has_next).astype(jnp.float32)
    offsets = jnp.array([0, 1, cols, cols + 1], dtype=jnp.int32)
    corners = target[None, :] + offsets[:, None]
    rim = passed_along(down[-1:, :], XY, 1)
    down_above = jnp.concatenate([rim, down[:-1]], 0)
    across_left = jnp.concatenate([jnp.zeros((rows, 1), jnp.float32), across[:, :-1]], 1)
    got_corners = passed_along(corners, GZ, 1)
    got_weights = passed_along(weights, GZ, 1)

    def springs(field):
        padded = padded_2(field, ((XY, 1),), 1)
        upper = padded[:, :-2]
        lower = padded[:, 2:]
        zero_col = jnp.zeros((2, rows, 1), jnp.float32)
        right = jnp.concatenate([field[:, :, 1:], zero_col], 2)
        left = jnp.concatenate([zero_col, field[:, :, :-1]], 2)
        return (
            across * (field - right)
            + across_left * (field - left)
            + down * (field - lower)
            + down_above * (field - upper)
            + hold * field
        )

    def links(field):
        flat = field.reshape(2, rows * cols)
        own_values = flat[:, source]
        empty = jnp.zeros((2, rows * cols), jnp.float32)
        interp_mine = jnp.sum(got_weights[None] * flat[:, got_corners], 1)
        interp = passed_along(interp_mine, GZ, -1)
        error = (interp - own_values) * live[None]
        error_in = passed_along(error, GZ, 1)
        onward = empty.at[:, got_corners.reshape(-1)].add(
            (got_weights[None] * error_in[:, None, :]).reshape(2, -1)
        )
        own = empty.at[:, source].add(-error)
        return (own + onward).reshape(2, rows, cols)

    def operate(field):
        return springs(field) + links(field)

    solution_field = jnp.zeros_like(rhs)
    residual = rhs
    image = operate(residual)
    norm_now, product = two_products(residual, image)
    alpha = norm_now / product
    direction, along = (residual, image)
    for step in range(ITERS):
        solution_field = solution_field + alpha * direction
        residual = residual - alpha * along
        if step + 1 < ITERS:
            image = operate(residual)
            norm_next, product = two_products(residual, image)
            ratio = norm_next / norm_now
            alpha = norm_next / (product - ratio * norm_next / alpha)
            direction = residual + ratio * direction
            along = image + ratio * along
            norm_now = norm_next
    return (solution_field[:, None], residual[:, None])


def solution(mesh):
    split = Mesh(mesh.devices.reshape(4, 16, 4, 2), ("gz_0", "gz_1", "xy_0", "xy_1"))
    in_specs = (
        P(None, GZ, XY, None),
        P(GZ, XY, None),
        P(GZ, XY, None),
        P(GZ, XY, None),
        P(GZ, XY, None),
        P(GZ, XY, None),
        P(None, GZ, XY, None),
        P(GZ, XY),
    )
    out_specs = (P(None, GZ, XY, None), P(None, GZ, XY, None))
    return jax.shard_map(body, mesh=split, in_specs=in_specs, out_specs=out_specs, check_vma=False)
```

profile of v0, /device:TPU:1, one launch (start us, length us, event | category | flops | bytes accessed | tf_op | source)
XLA Modules:
  0.0 437.7 jit_solution(2395866498176098867)
XLA Ops:
  23.8 5.5 %copy.51 = f32[2,1,8,2048]{0,3,2,1:T(8,128)} copy(f32[2,1,8,2048]{3,2,1,0:T(8,128)} %param.9) | data formatting | bytes 262144 | tf_op args[0]
  29.3 6.2 %gather_fusion.1 = f32[1024,2]{1,0:T(8,128)S(1)} fusion(f32[2,16384]{0,1:T(8,128)} %bitcast.83, s32[1024]{0:T(1024)S(1)} %broadcast_clamp_fusion), kind=kCustom, calls=%fused_computation.1 | custom fusion | bytes 20480 | tf_op jit(solution)/shard_map/gather | solution.py:98
  35.8 14.1 %gather_fusion = f32[4096,2]{1,0:T(8,128)S(1)} fusion(f32[2,16384]{0,1:T(8,128)} %bitcast.84, s32[4096]{0:T(1024)S(1)} %bitcast_clamp_fusion), kind=kCustom, calls=%fused_computation | custom fusion | bytes 81920 | tf_op jit(solution)/shard_map/gather | solution.py:100
  62.0 38.0 %scatter_custom_fusion = f32[2,16384]{0,1:T(8,128)} fusion(s32[5120]{0:T(1024)S(1)} %bitcast.115, f32[5120,2]{1,0:T(8,128)S(1)} %copy.54, f32[]{:T(128)} %constant.10.clone.1), kind=kCustom, calls=%fused_computation.13 | custom fusion | flops 10240 | bytes 131076 | tf_op jit(solution)/shard_map/add | solution.py:108
  100.0 5.3 %copy.55 = f32[2,8,2048]{2,1,0:T(8,128)S(1)} copy(f32[2,8,2048]{0,2,1:T(8,128)} %bitcast.81) | data formatting | bytes 262144 | tf_op jit(solution)/shard_map/reshape | solution.py:108
  106.0 8.1 %all-reduce.15 = (f32[]{:T(128)}, f32[]{:T(128)}) all-reduce(f32[]{:T(128)} %get-tuple-element.7, f32[]{:T(128)} %get-tuple-element.6), channel_id=1, replica_groups=mesh['gz_0'=4,'gz_1'=16,'xy_0'=4,'xy_1'=2] {'gz_0'}, use_global_device_ids=true, to_apply=%region_1.0 | all-reduce | flops 2 | bytes 16 | tf_op jit(solution)/shard_map/psum | solution.py:16
  114.1 21.8 %all-reduce.9 = (f32[]{:T(128)}, f32[]{:T(128)}) all-reduce(f32[]{:T(128)} %get-tuple-element.24, f32[]{:T(128)} %get-tuple-element.25), channel_id=1, replica_groups=mesh['gz_0'=4,'gz_1'=16,'xy_0'=4,'xy_1'=2] {'gz_1'}, use_global_device_ids=true, to_apply=%region_2.0 | all-reduce | flops 2 | bytes 16 | tf_op jit(solution)/shard_map/psum | solution.py:16
  136.0 7.8 %all-reduce.12 = (f32[]{:T(128)}, f32[]{:T(128)}) all-reduce(f32[]{:T(128)} %get-tuple-element.12, f32[]{:T(128)} %get-tuple-element.13), channel_id=1, replica_groups=mesh['gz_0'=4,'gz_1'=16,'xy_0'=4,'xy_1'=2] {'xy_0'}, use_global_device_ids=true, to_apply=%region_3.0 | all-reduce | flops 2 | bytes 16 | tf_op jit(solution)/shard_map/psum | solution.py:16
  143.8 16.2 %all-reduce.18 = (f32[]{:T(128)}, f32[]{:T(128)}) all-reduce(f32[]{:T(128)} %get-tuple-element.18, f32[]{:T(128)} %get-tuple-element.19), channel_id=1, replica_groups=mesh['gz_0'=4,'gz_1'=16,'xy_0'=4,'xy_1'=2] {'xy_1'}, use_global_device_ids=true, to_apply=%region_4.0 | all-reduce | flops 2 | bytes 16 | tf_op jit(solution)/shard_map/psum | solution.py:16
  165.9 14.1 %gather_fusion.2 = f32[4096,2]{1,0:T(8,128)S(1)} fusion(f32[2,16384]{0,1:T(8,128)} %bitcast.87, s32[4096]{0:T(1024)S(1)} %bitcast_clamp_fusion), kind=kCustom, calls=%fused_computation.2 | custom fusion | bytes 81920 | tf_op jit(solution)/shard_map/gather | solution.py:100
  183.1 6.2 %gather_fusion.3 = f32[1024,2]{1,0:T(8,128)S(1)} fusion(f32[2,16384]{0,1:T(8,128)} %bitcast.88, s32[1024]{0:T(1024)S(1)} %copy-done.13), kind=kCustom, calls=%fused_computation.3 | custom fusion | bytes 20480 | tf_op jit(solution)/shard_map/gather | solution.py:98
  200.0 38.1 %scatter_custom_fusion.1 = f32[2,16384]{0,1:T(8,128)} fusion(s32[5120]{0:T(1024)} %bitcast.116, f32[5120,2]{1,0:T(8,128)S(1)} %copy.59, f32[]{:T(128)} %constant.10.clone.1), kind=kCustom, calls=%fused_computation.11 | custom fusion | flops 10240 | bytes 131584 | tf_op jit(solution)/shard_map/add | solution.py:108
  245.5 6.7 %all-reduce.14 = (f32[]{:T(128)}, f32[]{:T(128)}) all-reduce(f32[]{:T(128)} %get-tuple-element.5, f32[]{:T(128)} %get-tuple-element.4), channel_id=1, replica_groups=mesh['gz_0'=4,'gz_1'=16,'xy_0'=4,'xy_1'=2] {'gz_0'}, use_global_device_ids=true, to_apply=%region_13.0 | all-reduce | flops 2 | bytes 16 | tf_op jit(solution)/shard_map/psum | solution.py:16
  252.3 20.7 %all-reduce.8 = (f32[]{:T(128)}, f32[]{:T(128)}) all-reduce(f32[]{:T(128)} %get-tuple-element.22, f32[]{:T(128)} %get-tuple-element.23), channel_id=1, replica_groups=mesh['gz_0'=4,'gz_1'=16,'xy_0'=4,'xy_1'=2] {'gz_1'}, use_global_device_ids=true, to_apply=%region_14.0 | all-reduce | flops 2 | bytes 16 | tf_op jit(solution)/shard_map/psum | solution.py:16
  272.9 6.9 %all-reduce.11 = (f32[]{:T(128)}, f32[]{:T(128)}) all-reduce(f32[]{:T(128)} %get-tuple-element.10, f32[]{:T(128)} %get-tuple-element.11), channel_id=1, replica_groups=mesh['gz_0'=4,'gz_1'=16,'xy_0'=4,'xy_1'=2] {'xy_0'}, use_global_device_ids=true, to_apply=%region_15.0 | all-reduce | flops 2 | bytes 16 | tf_op jit(solution)/shard_map/psum | solution.py:16
  279.8 13.2 %all-reduce.17 = (f32[]{:T(128)}, f32[]{:T(128)}) all-reduce(f32[]{:T(128)} %get-tuple-element.16, f32[]{:T(128)} %get-tuple-element.17), channel_id=1, replica_groups=mesh['gz_0'=4,'gz_1'=16,'xy_0'=4,'xy_1'=2] {'xy_1'}, use_global_device_ids=true, to_apply=%region_16.0 | all-reduce | flops 2 | bytes 16 | tf_op jit(solution)/shard_map/psum | solution.py:16
  302.3 14.1 %gather_fusion.4 = f32[4096,2]{1,0:T(8,128)S(1)} fusion(f32[2,16384]{0,1:T(8,128)} %bitcast.85, s32[4096]{0:T(1024)S(1)} %bitcast_clamp_fusion), kind=kCustom, calls=%fused_computation.4 | custom fusion | bytes 81920 | tf_op jit(solution)/shard_map/gather | solution.py:100
  319.4 6.7 %gather_fusion.5 = f32[1024,2]{1,0:T(8,128)S(1)} fusion(f32[2,16384]{0,1:T(8,128)} %bitcast.86, s32[1024]{0:T(1024)} %copy-done.12), kind=kCustom, calls=%fused_computation.5 | custom fusion | bytes 20480 | tf_op jit(solution)/shard_map/gather | solution.py:98
  340.4 38.1 %scatter_custom_fusion.2 = f32[2,16384]{0,1:T(8,128)} fusion(s32[5120]{0:T(1024)} %bitcast.117, f32[5120,2]{1,0:T(8,128)S(1)} %copy.64, f32[]{:T(128)} %constant.10.clone.1), kind=kCustom, calls=%fused_computation.9 | custom fusion | flops 10240 | bytes 131584 | tf_op jit(solution)/shard_map/add | solution.py:108
  378.5 5.3 %copy.65 = f32[2,8,2048]{2,1,0:T(8,128)S(1)} copy(f32[2,8,2048]{0,2,1:T(8,128)} %bitcast.80) | data formatting | bytes 262144 | tf_op jit(solution)/shard_map/reshape | solution.py:108
  385.3 6.6 %all-reduce.13 = (f32[]{:T(128)}, f32[]{:T(128)}) all-reduce(f32[]{:T(128)} %get-tuple-element.3, f32[]{:T(128)} %get-tuple-element.2), channel_id=1, replica_groups=mesh['gz_0'=4,'gz_1'=16,'xy_0'=4,'xy_1'=2] {'gz_0'}, use_global_device_ids=true, to_apply=%region_25.0 | all-reduce | flops 2 | bytes 16 | tf_op jit(solution)/shard_map/psum | solution.py:16
  391.9 21.0 %all-reduce.7 = (f32[]{:T(128)}, f32[]{:T(128)}) all-reduce(f32[]{:T(128)} %get-tuple-element.20, f32[]{:T(128)} %get-tuple-element.21), channel_id=1, replica_groups=mesh['gz_0'=4,'gz_1'=16,'xy_0'=4,'xy_1'=2] {'gz_1'}, use_global_device_ids=true, to_apply=%region_26.0 | all-reduce | flops 2 | bytes 16 | tf_op jit(solution)/shard_map/psum | solution.py:16
  412.9 7.3 %all-reduce.10 = (f32[]{:T(128)}, f32[]{:T(128)}) all-reduce(f32[]{:T(128)} %get-tuple-element.8, f32[]{:T(128)} %get-tuple-element.9), channel_id=1, replica_groups=mesh['gz_0'=4,'gz_1'=16,'xy_0'=4,'xy_1'=2] {'xy_0'}, use_global_device_ids=true, to_apply=%region_27.0 | all-reduce | flops 2 | bytes 16 | tf_op jit(solution)/shard_map/psum | solution.py:16
  420.2 12.8 %all-reduce.16 = (f32[]{:T(128)}, f32[]{:T(128)}) all-reduce(f32[]{:T(128)} %get-tuple-element.14, f32[]{:T(128)} %get-tuple-element.15), channel_id=1, replica_groups=mesh['gz_0'=4,'gz_1'=16,'xy_0'=4,'xy_1'=2] {'xy_1'}, use_global_device_ids=true, to_apply=%region_28.0 | all-reduce | flops 2 | bytes 16 | tf_op jit(solution)/shard_map/psum | solution.py:16
  (121 shorter events, 85.0 us)
Async XLA Ops:
  1.4 34.4 %collective-permute-start.3 = (s32[4,1024]{1,0:T(4,128)S(1)}, s32[4,1024]{1,0:T(4,128)S(1)}, u32[]{:S(2)}, u32[]{:S(2)}) collective-permute-start(s32[4,1024]{1,0:T(4,128)S(1)} %broadcast_add_fusion), channel_id=1, source_target_pairs={{0,8},{8,16},{16,24},{24,32},{32,40},{40,48},{48,56},{56,64},{64,7... | collective-permute-start | bytes 49160 | tf_op jit(solution)/shard_map/ppermute | solution.py:23
  6.5 43.5 %collective-permute-start.4 = (f32[4,1024]{1,0:T(4,128)S(1)}, f32[4,1024]{1,0:T(4,128)S(1)}, u32[]{:S(2)}, u32[]{:S(2)}) collective-permute-start(f32[4,1024]{1,0:T(4,128)S(1)} %bitcast.118), channel_id=1, source_target_pairs={{0,8},{8,16},{16,24},{24,32},{32,40},{40,48},{48,56},{56,64},{64,7... | collective-permute-start | bytes 49160 | tf_op jit(solution)/shard_map/ppermute | solution.py:23
  11.1 94.2 %collective-permute-start = (f32[2,1,2048]{2,1,0:T(1,128)S(1)}, f32[2,1,2048]{2,1,0:T(1,128)S(1)}, u32[]{:S(2)}, u32[]{:S(2)}) collective-permute-start(f32[2,1,2048]{2,1,0:T(1,128)S(1)} %get-tuple-element.53), channel_id=1, source_target_pairs={{1,0},{2,1},{3,2},{4,3},{5,4},{6,5},{7,6},{9,8},{10,9},{11,10},{12... | collective-permute-start | bytes 49160 | tf_op jit(solution)/shard_map/ppermute | solution.py:36
  14.5 90.7 %collective-permute-start.2 = (f32[2,1,2048]{2,1,0:T(1,128)S(1)}, f32[2,1,2048]{2,1,0:T(1,128)S(1)}, u32[]{:S(2)}, u32[]{:S(2)}) collective-permute-start(f32[2,1,2048]{2,1,0:T(1,128)S(1)} %get-tuple-element.54), channel_id=1, source_target_pairs={{0,1},{1,2},{2,3},{3,4},{4,5},{5,6},{6,7},{8,9},{9,10},{10,11},{11... | collective-permute-start | bytes 49160 | tf_op jit(solution)/shard_map/ppermute | solution.py:34
  18.1 17.7 %collective-permute-start.1 = (f32[1,2048]{1,0:T(1,128)S(1)}, f32[1,2048]{1,0:T(1,128)S(1)}, u32[]{:S(2)}, u32[]{:S(2)}) collective-permute-start(f32[1,2048]{1,0:T(1,128)S(1)} %slice_bitcast_fusion.1), channel_id=1, source_target_pairs={{0,1},{1,2},{2,3},{3,4},{4,5},{5,6},{6,7},{8,9},{9,10},{10,11},{11... | collective-permute-start | bytes 24584 | tf_op jit(solution)/shard_map/ppermute | solution.py:23
  23.1 6.2 %copy-start.12 = (s32[1024]{0:T(1024)}, s32[1024]{0:T(1024)S(1)}, u32[]{:S(2)}) copy-start(s32[1024]{0:T(1024)S(1)} %broadcast_clamp_fusion) | copy-start | bytes 12292
  23.8 31.7 %copy-start.10 = (f32[1024]{0:T(1024)}, f32[1024]{0:T(1024)S(1)}, u32[]{:S(2)}) copy-start(f32[1024]{0:T(1024)S(1)} %fusion.35) | copy-start | bytes 12292
  23.8 11.9 %copy-start.2 = (f32[1,8,2048]{2,1,0:T(8,128)S(1)}, f32[1,8,2048]{2,1,0:T(8,128)}, u32[]{:S(2)}) copy-start(f32[1,8,2048]{2,1,0:T(8,128)} %param.10) | copy-start | bytes 196612
  50.9 4.6 %collective-permute-start.5 = (f32[2,1024]{1,0:T(2,128)S(1)}, f32[2,1024]{1,0:T(2,128)S(1)}, u32[]{:S(2)}, u32[]{:S(2)}) collective-permute-start(f32[2,1024]{1,0:T(2,128)S(1)} %bitcast.121), channel_id=1, source_target_pairs={{8,0},{16,8},{24,16},{32,24},{40,32},{48,40},{56,48},{64,56},{72,6... | collective-permute-start | bytes 24584 | tf_op jit(solution)/shard_map/ppermute | solution.py:23
  55.5 5.5 %collective-permute-start.6 = (f32[2,1024]{1,0:T(2,128)S(1)}, f32[2,1024]{1,0:T(2,128)S(1)}, u32[]{:S(2)}, u32[]{:S(2)}) collective-permute-start(f32[2,1024]{1,0:T(2,128)S(1)} %get-tuple-element.40), channel_id=1, source_target_pairs={{0,8},{8,16},{16,24},{24,32},{32,40},{40,48},{48,56},{56,64},{64,7... | collective-permute-start | bytes 24584 | tf_op jit(solution)/shard_map/ppermute | solution.py:23
  60.3 39.6 %copy-start.14 = (s32[5120,1]{0,1:T(1,128)}, s32[5120,1]{0,1:T(1,128)S(1)}, u32[]{:S(2)}) copy-start(s32[5120,1]{0,1:T(1,128)S(1)} %pad_add_fusion) | copy-start | bytes 61444
  60.3 138.8 %copy-start.9 = (f32[1,8,4,128]{3,1,2,0:T(8,128)}, f32[1,8,4,128]{3,1,2,0:T(8,128)S(1)}, u32[]{:S(2)}) copy-start(f32[1,8,4,128]{3,1,2,0:T(8,128)S(1)} %copy.76) | copy-start | bytes 49156
  165.9 17.1 %copy-start.13 = (s32[1024]{0:T(1024)S(1)}, s32[1024]{0:T(1024)}, u32[]{:S(2)}) copy-start(s32[1024]{0:T(1024)} %copy-done.12) | copy-start | bytes 12292
  165.9 23.5 %copy-start.11 = (f32[1024]{0:T(1024)S(1)}, f32[1024]{0:T(1024)}, u32[]{:S(2)}) copy-start(f32[1024]{0:T(1024)} %copy-done.10) | copy-start | bytes 12292
  181.0 8.4 %collective-permute-start.9 = (f32[2,1024]{1,0:T(2,128)S(1)}, f32[2,1024]{1,0:T(2,128)S(1)}, u32[]{:S(2)}, u32[]{:S(2)}) collective-permute-start(f32[2,1024]{1,0:T(2,128)S(1)} %bitcast.120), channel_id=1, source_target_pairs={{8,0},{16,8},{24,16},{32,24},{40,32},{48,40},{56,48},{64,56},{72,6... | collective-permute-start | bytes 24584 | tf_op jit(solution)/shard_map/ppermute | solution.py:23
  189.5 9.6 %collective-permute-start.10 = (f32[2,1024]{1,0:T(2,128)S(1)}, f32[2,1024]{1,0:T(2,128)S(1)}, u32[]{:S(2)}, u32[]{:S(2)}) collective-permute-start(f32[2,1024]{1,0:T(2,128)S(1)} %get-tuple-element.37), channel_id=1, source_target_pairs={{0,8},{8,16},{16,24},{24,32},{32,40},{40,48},{48,56},{56,64},{64,7... | collective-permute-start | bytes 24584 | tf_op jit(solution)/shard_map/ppermute | solution.py:23
  193.5 49.9 %collective-permute-start.7 = (f32[2,1,2048]{2,1,0:T(1,128)S(1)}, f32[2,1,2048]{2,1,0:T(1,128)S(1)}, u32[]{:S(2)}, u32[]{:S(2)}) collective-permute-start(f32[2,1,2048]{2,1,0:T(1,128)S(1)} %get-tuple-element.49), channel_id=1, source_target_pairs={{1,0},{2,1},{3,2},{4,3},{5,4},{6,5},{7,6},{9,8},{10,9},{11,10},{12... | collective-permute-start | bytes 49160 | tf_op jit(solution)/shard_map/ppermute | solution.py:36
  196.3 47.1 %collective-permute-start.8 = (f32[2,1,2048]{2,1,0:T(1,128)S(1)}, f32[2,1,2048]{2,1,0:T(1,128)S(1)}, u32[]{:S(2)}, u32[]{:S(2)}) collective-permute-start(f32[2,1,2048]{2,1,0:T(1,128)S(1)} %get-tuple-element.50), channel_id=1, source_target_pairs={{0,1},{1,2},{2,3},{3,4},{4,5},{5,6},{6,7},{8,9},{9,10},{10,11},{11... | collective-permute-start | bytes 49160 | tf_op jit(solution)/shard_map/ppermute | solution.py:34
  238.1 5.9 %copy-start.7 = (f32[2,8,2047]{2,1,0:T(8,128)S(1)}, f32[2,8,2047]{2,1,0:T(8,128)}, u32[]{:S(2)}) copy-start(f32[2,8,2047]{2,1,0:T(8,128)} %get-tuple-element.47) | copy-start | bytes 393028
  238.1 5.9 %copy-start.8 = (f32[2,8,2047]{2,1,0:T(8,128)S(1)}, f32[2,8,2047]{2,1,0:T(8,128)}, u32[]{:S(2)}) copy-start(f32[2,8,2047]{2,1,0:T(8,128)} %get-tuple-element.48) | copy-start | bytes 393028
  317.3 8.9 %collective-permute-start.13 = (f32[2,1024]{1,0:T(2,128)S(1)}, f32[2,1024]{1,0:T(2,128)S(1)}, u32[]{:S(2)}, u32[]{:S(2)}) collective-permute-start(f32[2,1024]{1,0:T(2,128)S(1)} %bitcast.119), channel_id=1, source_target_pairs={{8,0},{16,8},{24,16},{32,24},{40,32},{48,40},{56,48},{64,56},{72,6... | collective-permute-start | bytes 24584 | tf_op jit(solution)/shard_map/ppermute | solution.py:23
  327.0 10.5 %collective-permute-start.14 = (f32[2,1024]{1,0:T(2,128)S(1)}, f32[2,1024]{1,0:T(2,128)S(1)}, u32[]{:S(2)}, u32[]{:S(2)}) collective-permute-start(f32[2,1024]{1,0:T(2,128)S(1)} %get-tuple-element.34), channel_id=1, source_target_pairs={{0,8},{8,16},{16,24},{24,32},{32,40},{40,48},{48,56},{56,64},{64,7... | collective-permute-start | bytes 24584 | tf_op jit(solution)/shard_map/ppermute | solution.py:23
  331.9 51.9 %collective-permute-start.11 = (f32[2,1,2048]{2,1,0:T(1,128)}, f32[2,1,2048]{2,1,0:T(1,128)S(1)}, u32[]{:S(2)}, u32[]{:S(2)}) collective-permute-start(f32[2,1,2048]{2,1,0:T(1,128)} %get-tuple-element.45), channel_id=1, source_target_pairs={{1,0},{2,1},{3,2},{4,3},{5,4},{6,5},{7,6},{9,8},{10,9},{11,10},{12... | collective-permute-start | bytes 49160 | tf_op jit(solution)/shard_map/ppermute | solution.py:36
  334.4 49.4 %collective-permute-start.12 = (f32[2,1,2048]{2,1,0:T(1,128)}, f32[2,1,2048]{2,1,0:T(1,128)}, u32[]{:S(2)}, u32[]{:S(2)}) collective-permute-start(f32[2,1,2048]{2,1,0:T(1,128)} %get-tuple-element.46), channel_id=1, source_target_pairs={{0,1},{1,2},{2,3},{3,4},{4,5},{5,6},{6,7},{8,9},{9,10},{10,11},{11... | collective-permute-start | bytes 49160 | tf_op jit(solution)/shard_map/ppermute | solution.py:34
  (8 other events, 33.1 us)
where the time goes:
time: 440 us; the launch traced here: 438 us
  blocking collectives  149 us (34%)
  other arithmetic  125 us (28%)
  local copies, waits for them, and re-layouts  104 us (24%)
  starting transfers between devices  44.4 us (10%)
  between operations  11.8 us (3%)
    psum x12, blocking collectives, one_axis_at_a_time(): shard = lax.psum(shard, axis)  149 us
    add x3, other arithmetic, links(): return (own + onward).reshape(2, rows, cols)  114 us
    gather x3, local copies, waits for them, and re-layouts, links(): interp_mine = jnp.sum(got_weights[None] * flat[:, got_corners], 1)  42.4 us
    ppermute x9, starting transfers between devices, passed_along(): return lax.ppermute(block, axis, route)  27.1 us
    gather x6, local copies, waits for them, and re-layouts, links(): own_values = flat[:, source]  19.6 us
    reshape x3, local copies, waits for them, and re-layouts, links(): return (own + onward).reshape(2, rows, cols)  15.8 us
    sub x2, local copies, waits for them, and re-layouts, body(): residual = residual - alpha * along  9.15 us
  transfers between devices with their start and end apart: 15, of which 2 were waited for; matrix products, arithmetic and copies ran while one was open for 42% of the time, Pallas kernels for 0%

commit v1 on v0

v1 whole, which is shorter than its diff:
```python
import functools

import jax
import jax.numpy as jnp
from jax import lax
from jax.experimental import pallas as pl
from jax.experimental.pallas import tpu as pltpu
from jax.sharding import PartitionSpec as P

BLOCK = 128
ITERS = 3
LOW = 256
SCALE = 8.0
MESH = pl.DeviceIdType.MESH
MOMENTS = 2 * ITERS


def pieces(values, count):
    out = []
    for i in range(count):
        part = values.astype(jnp.bfloat16)
        out.append(part)
        if i + 1 < count:
            values = values - part.astype(jnp.float32)
    return jnp.concatenate(out, 0)


def summed(pieces_of, count):
    rows = pieces_of.shape[0] // count
    total = pieces_of[:rows]
    for i in range(1, count):
        total = total + pieces_of[i * rows : (i + 1) * rows]
    return total


def stacked(field):
    return jnp.concatenate(
        [part[:, h : h + LOW] for part in field for h in range(0, part.shape[1], LOW)], 0
    )


def unstacked(table, rows, highs):
    return [
        jnp.concatenate(
            [table[(c * highs + h) * rows : (c * highs + h + 1) * rows] for h in range(highs)], 1
        )
        for c in range(2)
    ]


def looked_up(table, hot, masks, first):
    wide = hot.shape[1]
    cut = min(wide, 256)
    out = []
    for j in range(0, wide, cut):
        found = jnp.dot(table, hot[:, j : j + cut], preferred_element_type=jnp.float32)
        out.append([])
        per = found.shape[0] // len(masks)
        totals = None
        for m, mask in enumerate(masks):
            got = summed(found[m * per : (m + 1) * per], first)
            half = got.shape[0] // 2
            terms = [got[c * half : (c + 1) * half] * mask[:, j : j + cut] for c in range(2)]
            totals = terms if totals is None else [a + b for a, b in zip(totals, terms)]
        out[-1] = [jnp.sum(t, 0, keepdims=True) for t in totals]
    return [jnp.concatenate([o[c] for o in out], 1) for c in range(2)]


def spread(errors, mask, hot, count):
    table = jnp.concatenate([mask[...] * e for e in errors], 0)
    out = lax.dot_general(
        pieces(table, count), hot[...], (((1,), (1,)), ((), ())), preferred_element_type=jnp.float32
    )
    return summed(out, count)


def folded(values):
    return sum(values[:, i : i + 128] for i in range(0, values.shape[1], 128))


def coefficients(mu):
    def inner(a, b, shift):
        total = None
        for i, x in enumerate(a):
            for j, y in enumerate(b):
                term = mu[i + j + shift]
                if x is not None:
                    term = x * term
                if y is not None:
                    term = y * term
                total = term if total is None else total + term
        return total

    residual, direction, field = [None], [None], []
    norm = mu[0]
    for step in range(ITERS):
        alpha = norm / inner(direction, direction, 1)
        along = [alpha if d is None else alpha * d for d in direction]
        field = [a if i >= len(field) else field[i] + a for i, a in enumerate(along)]
        residual = residual[:1] + [
            -a if i + 1 >= len(residual) else residual[i + 1] - a for i, a in enumerate(along)
        ]
        if step + 1 < ITERS:
            fresh = inner(residual, residual, 0)
            ratio = fresh / norm
            step_of = [ratio if d is None else ratio * d for d in direction]
            direction = [
                (1.0 if r is None else r) + (step_of[i] if i < len(step_of) else 0.0)
                for i, r in enumerate(residual)
            ]
            norm = fresh
    return field, residual


def kernel(
    ny,
    nz,
    nx,
    rhs_ref,
    across_ref,
    down_ref,
    anchor_ref,
    source_ref,
    target_ref,
    weight_ref,
    count_ref,
    x_ref,
    r_ref,
    hot_source,
    hot_target,
    mask_source,
    mask_left,
    mask_right,
    basis,
    weight_out,
    rim_out,
    halo_out,
    point_out,
    target_in,
    weight_in,
    rim_in,
    halo_in,
    point_in,
    sums,
    send_sem,
    recv_sem,
):
    rows, cols = across_ref.shape[1:]
    slots = source_ref.shape[2]
    highs = cols // LOW
    bits_cols, bits_low = cols.bit_length() - 1, LOW.bit_length() - 1
    n_gz = ny * nz
    gz, xy = lax.axis_index("gz"), lax.axis_index("xy")
    y, z = gz // nz, gz % nz
    after, before = ((gz + 1) % n_gz, xy), ((gz + n_gz - 1) % n_gz, xy)
    below, above = (gz, (xy + 1) % nx), (gz, (xy + nx - 1) % nx)

    groups = [[], [], []]
    for i in range(1, nx):
        groups[0].append((gz, (xy + i) % nx))
    for i in range(1, 2 * ny):
        groups[1].append((((y + i // 2) % ny) * nz + z - z % 2 + (z % 2 + i % 2) % 2, xy))
    for i in range(1, nz // 2):
        groups[2].append((y * nz + (z + 2 * i) % nz, xy))

    barrier = pltpu.get_barrier_semaphore()
    met = [after, before] + [peer for group in groups for peer in group]
    for peer in met:
        pl.semaphore_signal(barrier, inc=1, device_id=peer, device_id_type=MESH)

    sent = []

    def send(src, dst, peer, index):
        copy = pltpu.make_async_remote_copy(
            src_ref=src,
            dst_ref=dst,
            send_sem=send_sem.at[index],
            recv_sem=recv_sem.at[index],
            device_id=peer,
            device_id_type=MESH,
        )
        copy.start()
        sent.append(copy)
        return copy

    slot = lax.broadcasted_iota(jnp.int32, (1, slots), 1)
    live = ((slot < count_ref[0, 0] * BLOCK) & (gz < n_gz - 1)).astype(jnp.float32)
    for k in range(4):
        weight_out[k] = weight_ref[k, 0] * live
    rim_out[...] = down_ref[0, rows - 1 :]

    def post_halo(field, k):
        for c in range(2):
            halo_out[k, 0, c : c + 1, :] = field[c][:1]
            halo_out[k, 1, c : c + 1, :] = field[c][rows - 1 :]

    field = [rhs_ref[c, 0] for c in range(2)]
    post_halo(field, 0)

    low_id = lax.broadcasted_iota(jnp.int32, (LOW, slots), 0)
    place_id = lax.broadcasted_iota(jnp.int32, (highs * rows, slots), 0)

    def split(node):
        col = node & (cols - 1)
        return col & (LOW - 1), (col >> bits_low) * rows + (node >> bits_cols)

    low, place = split(source_ref[0])
    hot_source[...] = (low_id == low).astype(jnp.float32).astype(jnp.bfloat16)
    mask_source[...] = jnp.where(place_id == place, live, 0.0)

    pl.semaphore_wait(barrier, len(met))

    copies = [
        send(target_ref, target_in, after, 0),
        send(weight_out, weight_in, after, 1),
        send(rim_out, rim_in, below, 2),
    ]
    across, down, anchor = across_ref[0], down_ref[0], anchor_ref[0]
    col_id = lax.broadcasted_iota(jnp.int32, (rows, cols), 1)
    row_id = lax.broadcasted_iota(jnp.int32, (rows, cols), 0)
    products = [sum(folded(f * f) for f in field)]

    for k in range(ITERS):
        base = 3 + 4 * k
        halo = [
            send(halo_out.at[k, 0], halo_in.at[k, 0], above, base),
            send(halo_out.at[k, 1], halo_in.at[k, 1], below, base + 1),
        ]
        own = looked_up(pieces(stacked(field), 3), hot_source, [mask_source], 3)
        for c in range(2):
            point_out[k, 0, c : c + 1, :] = own[c]
        own_copy = send(point_out.at[k, 0], point_in.at[k, 0], after, base + 2)
        right = [jnp.where(col_id == cols - 1, 0.0, pltpu.roll(f, cols - 1, 1)) for f in field]
        if k == 0:
            copies[0].wait_recv()
            copies[1].wait_recv()
            low, place = split(target_in[0])
            hot_target[...] = (low_id == low).astype(jnp.float32).astype(jnp.bfloat16)
            for mask, one, two in ((mask_left, 0, 2), (mask_right, 1, 3)):
                mask[...] = jnp.where(
                    place_id == place,
                    weight_in[one],
                    jnp.where(place_id == place + 1, weight_in[two], 0.0),
                )
        table = jnp.concatenate([pieces(stacked(field), 3), pieces(stacked(right), 3)], 0)
        there = looked_up(table, hot_target, [mask_left, mask_right], 3)
        for c in range(2):
            point_out[k, 1, c : c + 1, :] = there[c]
        there_copy = send(point_out.at[k, 1], point_in.at[k, 1], before, base + 3)

        if k == 0:
            copies[2].wait_recv()
        halo[0].wait_recv()
        halo[1].wait_recv()
        image, energy = [], None
        for c in range(2):
            f = field[c]
            upper = jnp.where(xy > 0, halo_in[k, 1, c : c + 1, :], 0.0)
            lower = jnp.where(xy < nx - 1, halo_in[k, 0, c : c + 1, :], 0.0)
            rim = jnp.where(xy > 0, rim_in[...], 0.0)
            gap = f - right[c]
            flux = across * gap
            fall = f - jnp.where(row_id == rows - 1, lower, pltpu.roll(f, rows - 1, 0))
            drop = down * fall
            held = anchor * f
            come = jnp.where(col_id == 0, 0.0, pltpu.roll(flux, 1, 1))
            down_in = jnp.where(row_id == 0, rim * (upper - f), pltpu.roll(drop, 1, 0))
            image.append(flux - come + drop - down_in + held)
            if k == ITERS - 1:
                term = flux * gap + drop * fall + held * f
                energy = term if energy is None else energy + term

        own_copy.wait_recv()
        error_in = [there[c] - point_in[k, 0, c : c + 1, :] for c in range(2)]

        def onward():
            left = unstacked(spread(error_in, mask_left, hot_target, 2), rows, highs)
            more = unstacked(spread(error_in, mask_right, hot_target, 2), rows, highs)
            return [a + pltpu.roll(b, 1, 1) for a, b in zip(left, more)]

        if k < ITERS - 1:
            image = [a + b for a, b in zip(image, onward())]
        there_copy.wait_recv()
        error = [point_in[k, 1, c : c + 1, :] - own[c] for c in range(2)]
        if k == ITERS - 1:
            tie = sum(e * e for e in error)
            last = folded(energy) * (1.0 / SCALE)
            last_tie = folded(tie) * (1.0 / SCALE)
            products.append(last)
            lanes = jnp.concatenate([jnp.sum(p, 0, keepdims=True) for p in products], 0)
            lanes = jnp.concatenate([lanes, jnp.zeros((8 - MOMENTS, 128), jnp.float32)], 0)
            eight = lax.broadcasted_iota(jnp.int32, (8, 128), 0)
            lanes = lanes + jnp.where(eight == MOMENTS - 1, last_tie, 0.0)
            total = jnp.sum(lanes, 1, keepdims=True)
            lane = lax.broadcasted_iota(jnp.int32, (8, 128), 1)
            total = jnp.sum(jnp.where(lane == eight, total, 0.0), 0, keepdims=True)

        def post_sum(stage, total):
            sums[stage, 0] = total
            index = 3 + 4 * ITERS + stage
            for i, peer in enumerate(groups[stage]):
                copy = pltpu.make_async_remote_copy(
                    src_ref=sums.at[stage, 0],
                    dst_ref=sums.at[stage, i + 1],
                    send_sem=send_sem.at[index],
                    recv_sem=recv_sem.at[index],
                    device_id=peer,
                    device_id_type=MESH,
                )
                copy.start()

        def take_sum(stage):
            index = 3 + 4 * ITERS + stage
            count = len(groups[stage])
            arrived = sums.at[stage, pl.ds(1, count)]
            pltpu.make_async_copy(arrived, arrived, recv_sem.at[index]).wait()
            return functools.reduce(lambda a, b: a + b, [sums[stage, i] for i in range(count + 1)])

        if k == ITERS - 1:
            post_sum(0, total)
            image = [a + b for a, b in zip(image, onward())]
        back = unstacked(spread(error, mask_source, hot_source, 2), rows, highs)
        latest = [(a - b) * (1.0 / SCALE) for a, b in zip(image, back)]
        if k < ITERS - 1:
            post_halo(latest, k + 1)
            products.append(sum(folded(a * b) for a, b in zip(field, latest)))
            products.append(sum(folded(a * a) for a in latest))
        for c in range(2):
            basis[k, c] = latest[c]
        field = latest

    for stage in (1, 2):
        total = take_sum(stage - 1)
        post_sum(stage, total)
    total = take_sum(2)
    lane = lax.broadcasted_iota(jnp.int32, (1, 128), 1)
    mu = [
        jnp.sum(jnp.where(lane == i, total, 0.0), 1, keepdims=True) for i in range(MOMENTS)
    ]
    steps, rest = coefficients(mu)
    for c in range(2):
        powers = [rhs_ref[c, 0]] + [basis[i, c] for i in range(ITERS)]
        x_ref[c, 0] = sum((s * (1.0 / SCALE)) * v for s, v in zip(steps, powers))
        r_ref[c, 0] = sum((v if s is None else s * v) for s, v in zip(rest, powers))

    for copy in sent:
        copy.wait_send()
    for stage in range(3):
        count = len(groups[stage])
        gone = sums.at[stage, pl.ds(1, count)]
        pltpu.make_async_copy(gone, gone, send_sem.at[3 + 4 * ITERS + stage]).wait()


def body(nz, rhs, across, down, anchor, source, target, weight, count):
    n_gz, nx = lax.axis_size("gz"), lax.axis_size("xy")
    ny = n_gz // nz
    rows, cols = across.shape[1:]
    slots = source.shape[2]
    places = rows * cols // LOW
    f32, bf16 = jnp.float32, jnp.bfloat16
    vmem = pl.BlockSpec(memory_space=pltpu.VMEM)
    smem = pl.BlockSpec(memory_space=pltpu.SMEM)
    out = jax.ShapeDtypeStruct(rhs.shape, f32)
    copies = 3 + 4 * ITERS + 3
    widest = max(nx, 2 * ny, nz // 2)
    return pl.pallas_call(
        functools.partial(kernel, ny, nz, nx),
        out_shape=(out, out),
        in_specs=[vmem] * 7 + [smem],
        out_specs=(vmem, vmem),
        scratch_shapes=[
            pltpu.VMEM((LOW, slots), bf16),
            pltpu.VMEM((LOW, slots), bf16),
            pltpu.VMEM((places, slots), f32),
            pltpu.VMEM((places, slots), f32),
            pltpu.VMEM((places, slots), f32),
            pltpu.VMEM((ITERS, 2, rows, cols), f32),
            pltpu.VMEM((4, 1, slots), f32),
            pltpu.VMEM((1, cols), f32),
            pltpu.VMEM((ITERS, 2, 2, cols), f32),
            pltpu.VMEM((ITERS, 2, 2, slots), f32),
            pltpu.VMEM((1, 1, slots), jnp.int32),
            pltpu.VMEM((4, 1, slots), f32),
            pltpu.VMEM((1, cols), f32),
            pltpu.VMEM((ITERS, 2, 2, cols), f32),
            pltpu.VMEM((ITERS, 2, 2, slots), f32),
            pltpu.VMEM((3, widest, 1, 128), f32),
            pltpu.SemaphoreType.DMA((copies,)),
            pltpu.SemaphoreType.DMA((copies,)),
        ],
        compiler_params=pltpu.CompilerParams(
            collective_id=0, has_side_effects=True, vmem_limit_bytes=48 * 1024 * 1024
        ),
    )(rhs, across, down, anchor, source, target, weight, count)


def solution(mesh, nz=16):
    in_specs = (
        P(None, "gz", "xy", None),
        P("gz", "xy", None),
        P("gz", "xy", None),
        P("gz", "xy", None),
        P("gz", "xy", None),
        P("gz", "xy", None),
        P(None, "gz", "xy", None),
        P("gz", "xy"),
    )
    out_specs = (P(None, "gz", "xy", None), P(None, "gz", "xy", None))
    return jax.shard_map(
        functools.partial(body, nz), mesh=mesh, in_specs=in_specs, out_specs=out_specs, check_vma=False
    )
```

time: 440 us -> 56.7 us (0.13)
  blocking collectives: 149 us -> 0 us
  other arithmetic: 125 us -> 0 us
  local copies, waits for them, and re-layouts: 104 us -> 6.82 us
  Pallas kernels: 0 us -> 48 us
  starting transfers between devices: 44.4 us -> 0 us
  between operations: 11.8 us -> 1.3 us
    psum x12 -> x0, blocking collectives: 149 us -> none  [one_axis_at_a_time(): shard = lax.psum(shard, axis)]
    add x4 -> x0, other arithmetic: 115 us -> none  [the longest x3 114 us: links(): return (own + onward).reshape(2, rows, cols)]
    gather x9 -> x0, local copies, waits for them, and re-layouts: 62 us -> none  [the longest x3 42.4 us: links(): interp_mine = jnp.sum(got_weights[None] * flat[:, got_corners], 1)]
    pallas_call x0 -> x1, Pallas kernels: none -> 48 us  [body(): pl.pallas_call(functools.partial(kernel, ny, nz, nx), out_shape=(out, out...]
    ppermute x15 -> x0, starting transfers between devices: 44.4 us -> none  [the longest x9 27.1 us: passed_along(): return lax.ppermute(block, axis, route)]
    reshape x3 -> x0, local copies, waits for them, and re-layouts: 15.8 us -> none  [links(): return (own + onward).reshape(2, rows, cols)]
    sub x2 -> x0, local copies, waits for them, and re-layouts: 9.15 us -> none  [body(): residual = residual - alpha * along]
    slice x8 -> x0, local copies, waits for them, and re-layouts: 5.97 us -> none  [the longest x3 2.59 us: springs(): right = jnp.concatenate([field[:, :, 1:], zero_col], 2)]
  transfers between devices with their start and end apart: 15 -> 0, of which waited for: 2 -> 0; matrix products, arithmetic and copies ran while one was open for 42% -> 0% of each run, Pallas kernels for 0% -> 0%
where the time goes in v1:
time: 56.7 us; the launch traced here: 56.1 us
  Pallas kernels  48 us (85%)
  local copies, waits for them, and re-layouts  6.82 us (12%)
  between operations  1.3 us (2%)
    pallas_call x1, Pallas kernels, body(): pl.pallas_call(functools.partial(kernel, ny, nz, nx), out_shape=(out, out...  48 us
    unnamed x16, local copies, waits for them, and re-layouts  6.82 us

profile of v1, /device:TPU:1, one launch (start us, length us, event | category | flops | bytes accessed | tf_op | source)
XLA Modules:
  0.0 56.1 jit_solution(10623977381225662621)
XLA Ops:
  1.3 0.0 copy-start
  1.3 0.9 %copy-done = f32[2,1,8,2048]{3,2,1,0:T(8,128)S(1)} copy-done((f32[2,1,8,2048]{3,2,1,0:T(8,128)S(1)}, f32[2,1,8,2048]{3,2,1,0:T(8,128)}, u32[]{:S(2)}) %copy-start) | copy-done | bytes 131096
  2.2 0.0 copy-start.1
  2.2 0.8 %copy-done.1 = f32[1,8,2048]{2,1,0:T(8,128)S(1)} copy-done((f32[1,8,2048]{2,1,0:T(8,128)S(1)}, f32[1,8,2048]{2,1,0:T(8,128)}, u32[]{:S(2)}) %copy-start.1) | copy-done | bytes 65560
  3.0 0.0 copy-start.2
  3.0 0.8 %copy-done.2 = f32[1,8,2048]{2,1,0:T(8,128)S(1)} copy-done((f32[1,8,2048]{2,1,0:T(8,128)S(1)}, f32[1,8,2048]{2,1,0:T(8,128)}, u32[]{:S(2)}) %copy-start.2) | copy-done | bytes 65560
  3.9 0.0 copy-start.3
  3.9 0.8 %copy-done.3 = f32[1,8,2048]{2,1,0:T(8,128)S(1)} copy-done((f32[1,8,2048]{2,1,0:T(8,128)S(1)}, f32[1,8,2048]{2,1,0:T(8,128)}, u32[]{:S(2)}) %copy-start.3) | copy-done | bytes 65560
  4.7 0.0 copy-start.4
  4.7 0.7 %copy-done.4 = f32[4,1,1,1024]{3,2,1,0:T(1,128)S(1)} copy-done((f32[4,1,1,1024]{3,2,1,0:T(1,128)S(1)}, f32[4,1,1,1024]{3,2,1,0:T(1,128)}, u32[]{:S(2)}) %copy-start.4) | copy-done | bytes 16408
  5.4 0.0 copy-start.5
  5.4 0.7 %copy-done.5 = s32[1,1,1024]{2,1,0:T(1,128)S(1)} copy-done((s32[1,1,1024]{2,1,0:T(1,128)S(1)}, s32[1,1,1024]{2,1,0:T(1,128)}, u32[]{:S(2)}) %copy-start.5) | copy-done | bytes 4120
  6.1 0.0 copy-start.6
  6.1 0.7 %copy-done.6 = s32[1,1,1024]{2,1,0:T(1,128)S(1)} copy-done((s32[1,1,1024]{2,1,0:T(1,128)S(1)}, s32[1,1,1024]{2,1,0:T(1,128)}, u32[]{:S(2)}) %copy-start.6) | copy-done | bytes 4120
  6.8 48.0 %shard_map.95 = (f32[2,1,8,2048]{3,2,1,0:T(8,128)S(1)}, f32[2,1,8,2048]{3,2,1,0:T(8,128)S(1)}) custom-call(f32[2,1,8,2048]{3,2,1,0:T(8,128)S(1)} %copy-done, f32[1,8,2048]{2,1,0:T(8,128)S(1)} %copy-done.1, f32[1,8,2048]{2,1,0:T(8,128)S(1)} %copy-done.2, f32[1,8,2048]{2,1,0:T(8,128)S(1)} %copy-done.3, s32[1,1,1024]{2,1,0:T(1,128)S(1)} %copy-done.5, ...), custom_call_target="tpu_custom_call" | custom-call | tf_op jit(solution)/shard_map/pallas_call | solution.py:366
  54.8 0.7 %copy.13 = f32[2,1,8,2048]{3,2,1,0:T(8,128)} copy(f32[2,1,8,2048]{3,2,1,0:T(8,128)S(1)} %get-tuple-element.4) | data formatting | bytes 262144
  55.4 0.7 %copy.14 = f32[2,1,8,2048]{3,2,1,0:T(8,128)} copy(f32[2,1,8,2048]{3,2,1,0:T(8,128)S(1)} %get-tuple-element.5) | data formatting | bytes 262144
Async XLA Ops:
  1.3 0.9 %copy-start = (f32[2,1,8,2048]{3,2,1,0:T(8,128)S(1)}, f32[2,1,8,2048]{3,2,1,0:T(8,128)}, u32[]{:S(2)}) copy-start(f32[2,1,8,2048]{3,2,1,0:T(8,128)} %rhs_ref.1) | copy-start | bytes 393220
  2.2 0.8 %copy-start.1 = (f32[1,8,2048]{2,1,0:T(8,128)S(1)}, f32[1,8,2048]{2,1,0:T(8,128)}, u32[]{:S(2)}) copy-start(f32[1,8,2048]{2,1,0:T(8,128)} %across_ref.1) | copy-start | bytes 196612
  3.0 0.8 %copy-start.2 = (f32[1,8,2048]{2,1,0:T(8,128)S(1)}, f32[1,8,2048]{2,1,0:T(8,128)}, u32[]{:S(2)}) copy-start(f32[1,8,2048]{2,1,0:T(8,128)} %down_ref.1) | copy-start | bytes 196612
  3.9 0.8 %copy-start.3 = (f32[1,8,2048]{2,1,0:T(8,128)S(1)}, f32[1,8,2048]{2,1,0:T(8,128)}, u32[]{:S(2)}) copy-start(f32[1,8,2048]{2,1,0:T(8,128)} %anchor_ref.1) | copy-start | bytes 196612
  4.7 0.7 %copy-start.4 = (f32[4,1,1,1024]{3,2,1,0:T(1,128)S(1)}, f32[4,1,1,1024]{3,2,1,0:T(1,128)}, u32[]{:S(2)}) copy-start(f32[4,1,1,1024]{3,2,1,0:T(1,128)} %weight_ref.1) | copy-start | bytes 49156
  5.4 0.7 %copy-start.5 = (s32[1,1,1024]{2,1,0:T(1,128)S(1)}, s32[1,1,1024]{2,1,0:T(1,128)}, u32[]{:S(2)}) copy-start(s32[1,1,1024]{2,1,0:T(1,128)} %source_ref.1) | copy-start | bytes 12292
  6.1 0.7 %copy-start.6 = (s32[1,1,1024]{2,1,0:T(1,128)S(1)}, s32[1,1,1024]{2,1,0:T(1,128)}, u32[]{:S(2)}) copy-start(s32[1,1,1024]{2,1,0:T(1,128)} %target_ref.1) | copy-start | bytes 12292

commit v2 on v1

--- a/solution.py
+++ b/solution.py
@@ -116,22 +116,28 @@
     ny,
     nz,
     nx,
+    rhs_hbm,
+    across_hbm,
+    down_hbm,
+    anchor_hbm,
+    source_hbm,
+    target_hbm,
+    weight_hbm,
+    count_hbm,
+    basis,
+    scalars,
     rhs_ref,
     across_ref,
     down_ref,
     anchor_ref,
     source_ref,
-    target_ref,
     weight_ref,
     count_ref,
-    x_ref,
-    r_ref,
     hot_source,
     hot_target,
     mask_source,
     mask_left,
     mask_right,
-    basis,
     weight_out,
     rim_out,
     halo_out,
@@ -144,6 +150,8 @@
     sums,
     send_sem,
     recv_sem,
+    load_sem,
+    greet_sem,
 ):
     rows, cols = across_ref.shape[1:]
     slots = source_ref.shape[2]
@@ -151,22 +159,57 @@
     bits_cols, bits_low = cols.bit_length() - 1, LOW.bit_length() - 1
     n_gz = ny * nz
     gz, xy = lax.axis_index("gz"), lax.axis_index("xy")
-    y, z = gz // nz, gz % nz
+    y, z, x, core = gz // nz, gz % nz, xy // 2, xy % 2
     after, before = ((gz + 1) % n_gz, xy), ((gz + n_gz - 1) % n_gz, xy)
     below, above = (gz, (xy + 1) % nx), (gz, (xy + nx - 1) % nx)
 
-    groups = [[], [], []]
-    for i in range(1, nx):
-        groups[0].append((gz, (xy + i) % nx))
-    for i in range(1, 2 * ny):
-        groups[1].append((((y + i // 2) % ny) * nz + z - z % 2 + (z % 2 + i % 2) % 2, xy))
-    for i in range(1, nz // 2):
-        groups[2].append((y * nz + (z + 2 * i) % nz, xy))
+    def peers(offsets):
+        sizes = (ny, nz, nx // 2, 2)
+        kept = []
+        for offset in offsets:
+            offset = tuple(o % n for o, n in zip(offset, sizes))
+            if any(offset) and offset not in kept:
+                kept.append(offset)
+        return [
+            (((y + o[0]) % ny) * nz + (z + o[1]) % nz, ((x + o[2]) % (nx // 2)) * 2 + (core + o[3]) % 2)
+            for o in kept
+        ]
+
+    one_hop = peers(
+        [(0, 1, 0, 0), (0, -1, 0, 0), (1, 0, 0, 0), (-1, 0, 0, 0), (0, 0, 1, 0), (0, 0, -1, 0), (0, 0, 0, 1)]
+    )
+    two_hops = peers([(0, 2, 0, 0), (0, -2, 0, 0), (2, 0, 0, 0), (0, 0, 2, 0)])
+    four_hops = peers([(0, 4, 0, 0), (0, -4, 0, 0), (0, 0, 0, 1)])
+    plane = [(j, 0, i, c) for j in range(ny) for i in range(nx // 2) for c in range(2)]
+    line = [(0, i, 0, 0) for i in range(nz)]
+    far_first = lambda o: -sum(min(d, n - d) for d, n in zip(o, (ny, nz, nx // 2, 2)))
+    groups = [peers(sorted(plane, key=far_first)), peers(sorted(line, key=far_first))]
 
     barrier = pltpu.get_barrier_semaphore()
-    met = [after, before] + [peer for group in groups for peer in group]
+    met = [after, before, below, above] + one_hop
     for peer in met:
         pl.semaphore_signal(barrier, inc=1, device_id=peer, device_id_type=MESH)
+
+    def greet(stage, who):
+        for peer in who:
+            pl.semaphore_signal(greet_sem.at[stage], inc=1, device_id=peer, device_id_type=MESH)
+
+    loads = [
+        pltpu.make_async_copy(src, dst, load_sem.at[i])
+        for i, (src, dst) in enumerate(
+            [
+                (count_hbm, count_ref),
+                (weight_hbm, weight_ref),
+                (source_hbm, source_ref),
+                (rhs_hbm, rhs_ref),
+                (down_hbm, down_ref),
+                (across_hbm, across_ref),
+                (anchor_hbm, anchor_ref),
+            ]
+        )
+    ]
+    for load in loads:
+        load.start()
 
     sent = []
 
@@ -184,18 +227,33 @@
         return copy
 
     slot = lax.broadcasted_iota(jnp.int32, (1, slots), 1)
+    loads[0].wait()
+    loads[1].wait()
     live = ((slot < count_ref[0, 0] * BLOCK) & (gz < n_gz - 1)).astype(jnp.float32)
     for k in range(4):
         weight_out[k] = weight_ref[k, 0] * live
-    rim_out[...] = down_ref[0, rows - 1 :]
-
     def post_halo(field, k):
         for c in range(2):
             halo_out[k, 0, c : c + 1, :] = field[c][:1]
             halo_out[k, 1, c : c + 1, :] = field[c][rows - 1 :]
-
+        return [
+            send(halo_out.at[k, 0], halo_in.at[k, 0], above, 3 + 4 * k),
+            send(halo_out.at[k, 1], halo_in.at[k, 1], below, 4 + 4 * k),
+        ]
+
+    pl.semaphore_wait(barrier, len(met))
+    copies = [
+        send(target_hbm, target_in, after, 0),
+        send(weight_out, weight_in, after, 1),
+    ]
+    greet(0, one_hop)
+
+    loads[3].wait()
     field = [rhs_ref[c, 0] for c in range(2)]
-    post_halo(field, 0)
+    halo = post_halo(field, 0)
+    loads[4].wait()
+    rim_out[...] = down_ref[0, rows - 1 :]
+    copies.append(send(rim_out, rim_in, below, 2))
 
     low_id = lax.broadcasted_iota(jnp.int32, (LOW, slots), 0)
     place_id = lax.broadcasted_iota(jnp.int32, (highs * rows, slots), 0)
@@ -204,17 +262,14 @@
         col = node & (cols - 1)
         return col & (LOW - 1), (col >> bits_low) * rows + (node >> bits_cols)
 
+    loads[2].wait()
     low, place = split(source_ref[0])
     hot_source[...] = (low_id == low).astype(jnp.float32).astype(jnp.bfloat16)
     mask_source[...] = jnp.where(place_id == place, live, 0.0)
 
-    pl.semaphore_wait(barrier, len(met))
-
-    copies = [
-        send(target_ref, target_in, after, 0),
-        send(weight_out, weight_in, after, 1),
-        send(rim_out, rim_in, below, 2),
-    ]
+
+    loads[5].wait()
+    loads[6].wait()
     across, down, anchor = across_ref[0], down_ref[0], anchor_ref[0]
     col_id = lax.broadcasted_iota(jnp.int32, (rows, cols), 1)
     row_id = lax.broadcasted_iota(jnp.int32, (rows, cols), 0)
@@ -222,10 +277,6 @@
 
     for k in range(ITERS):
         base = 3 + 4 * k
-        halo = [
-            send(halo_out.at[k, 0], halo_in.at[k, 0], above, base),
-            send(halo_out.at[k, 1], halo_in.at[k, 1], below, base + 1),
-        ]
         own = looked_up(pieces(stacked(field), 3), hot_source, [mask_source], 3)
         for c in range(2):
             point_out[k, 0, c : c + 1, :] = own[c]
@@ -271,6 +322,12 @@
                 energy = term if energy is None else energy + term
 
         own_copy.wait_recv()
+        if k == 0:
+            pl.semaphore_wait(greet_sem.at[0], len(one_hop))
+            greet(1, two_hops)
+        if k == 1:
+            pl.semaphore_wait(greet_sem.at[1], len(two_hops))
+            greet(2, four_hops)
         error_in = [there[c] - point_in[k, 0, c : c + 1, :] for c in range(2)]
 
         def onward():
@@ -297,6 +354,8 @@
 
         def post_sum(stage, total):
             sums[stage, 0] = total
+            if stage == 0:
+                pl.semaphore_wait(greet_sem.at[2], len(four_hops))
             index = 3 + 4 * ITERS + stage
             for i, peer in enumerate(groups[stage]):
                 copy = pltpu.make_async_remote_copy(
@@ -322,30 +381,29 @@
         back = unstacked(spread(error, mask_source, hot_source, 2), rows, highs)
         latest = [(a - b) * (1.0 / SCALE) for a, b in zip(image, back)]
         if k < ITERS - 1:
-            post_halo(latest, k + 1)
+            halo = post_halo(latest, k + 1)
             products.append(sum(folded(a * b) for a, b in zip(field, latest)))
             products.append(sum(folded(a * a) for a in latest))
         for c in range(2):
             basis[k, c] = latest[c]
         field = latest
 
-    for stage in (1, 2):
-        total = take_sum(stage - 1)
-        post_sum(stage, total)
-    total = take_sum(2)
+    post_sum(1, take_sum(0))
+    total = take_sum(1)
     lane = lax.broadcasted_iota(jnp.int32, (1, 128), 1)
     mu = [
         jnp.sum(jnp.where(lane == i, total, 0.0), 1, keepdims=True) for i in range(MOMENTS)
     ]
     steps, rest = coefficients(mu)
-    for c in range(2):
-        powers = [rhs_ref[c, 0]] + [basis[i, c] for i in range(ITERS)]
-        x_ref[c, 0] = sum((s * (1.0 / SCALE)) * v for s, v in zip(steps, powers))
-        r_ref[c, 0] = sum((v if s is None else s * v) for s, v in zip(rest, powers))
+    scalars[...] = jnp.concatenate(
+        [jnp.broadcast_to(s, (1, 128)) for s in [s * (1.0 / SCALE) for s in steps] + rest[1:]]
+        + [jnp.zeros((8 - 2 * ITERS, 128), jnp.float32)],
+        0,
+    )
 
     for copy in sent:
         copy.wait_send()
-    for stage in range(3):
+    for stage in range(2):
         count = len(groups[stage])
         gone = sums.at[stage, pl.ds(1, count)]
         pltpu.make_async_copy(gone, gone, send_sem.at[3 + 4 * ITERS + stage]).wait()
@@ -359,22 +417,31 @@
     places = rows * cols // LOW
     f32, bf16 = jnp.float32, jnp.bfloat16
     vmem = pl.BlockSpec(memory_space=pltpu.VMEM)
-    smem = pl.BlockSpec(memory_space=pltpu.SMEM)
-    out = jax.ShapeDtypeStruct(rhs.shape, f32)
-    copies = 3 + 4 * ITERS + 3
-    widest = max(nx, 2 * ny, nz // 2)
-    return pl.pallas_call(
+    hbm = pl.BlockSpec(memory_space=pltpu.HBM)
+    args = (rhs, across, down, anchor, source, target, weight, count)
+    copies = 3 + 4 * ITERS + 2
+    widest = max(nx * ny, nz)
+    basis, scalars = pl.pallas_call(
         functools.partial(kernel, ny, nz, nx),
-        out_shape=(out, out),
-        in_specs=[vmem] * 7 + [smem],
+        out_shape=(
+            jax.ShapeDtypeStruct((ITERS, 2, rows, cols), f32),
+            jax.ShapeDtypeStruct((8, 128), f32),
+        ),
+        in_specs=[hbm] * len(args),
         out_specs=(vmem, vmem),
         scratch_shapes=[
+            pltpu.VMEM(rhs.shape, f32),
+            pltpu.VMEM(across.shape, f32),
+            pltpu.VMEM(down.shape, f32),
+            pltpu.VMEM(anchor.shape, f32),
+            pltpu.VMEM(source.shape, jnp.int32),
+            pltpu.VMEM(weight.shape, f32),
+            pltpu.SMEM(count.shape, jnp.int32),
             pltpu.VMEM((LOW, slots), bf16),
             pltpu.VMEM((LOW, slots), bf16),
             pltpu.VMEM((places, slots), f32),
             pltpu.VMEM((places, slots), f32),
             pltpu.VMEM((places, slots), f32),
-            pltpu.VMEM((ITERS, 2, rows, cols), f32),
             pltpu.VMEM((4, 1, slots), f32),
             pltpu.VMEM((1, cols), f32),
             pltpu.VMEM((ITERS, 2, 2, cols), f32),
@@ -384,14 +451,20 @@
             pltpu.VMEM((1, cols), f32),
             pltpu.VMEM((ITERS, 2, 2, cols), f32),
             pltpu.VMEM((ITERS, 2, 2, slots), f32),
-            pltpu.VMEM((3, widest, 1, 128), f32),
+            pltpu.VMEM((2, widest, 1, 128), f32),
             pltpu.SemaphoreType.DMA((copies,)),
             pltpu.SemaphoreType.DMA((copies,)),
+            pltpu.SemaphoreType.DMA((7,)),
+            pltpu.SemaphoreType.REGULAR((3,)),
         ],
         compiler_params=pltpu.CompilerParams(
             collective_id=0, has_side_effects=True, vmem_limit_bytes=48 * 1024 * 1024
         ),
-    )(rhs, across, down, anchor, source, target, weight, count)
+    )(*args)
+    powers = [rhs[:, 0]] + [basis[i] for i in range(ITERS)]
+    field = sum(scalars[i, 0] * powers[i] for i in range(ITERS))
+    residual = powers[0] + sum(scalars[ITERS + i, 0] * powers[1 + i] for i in range(ITERS))
+    return field[:, None], residual[:, None]
 
 
 def solution(mesh, nz=16):

time: 56.7 us -> 54.8 us (0.966)
  Pallas kernels: 48 us -> 42.5 us
  other arithmetic: 0 us -> 4.45 us
  local copies, waits for them, and re-layouts: 6.82 us -> 6.1 us
    pallas_call x1, Pallas kernels: 48 us -> 42.5 us  [body(): pl.pallas_call(functools.partial(kernel, ny, nz, nx), out_shape=(jax.Shap...]
    unnamed x0 -> x1, other arithmetic: none -> 4.45 us
    unnamed x16 -> x14, local copies, waits for them, and re-layouts: 6.82 us -> 5.5 us
    slice x0 -> x1, local copies, waits for them, and re-layouts: none -> 0.6 us  [body(): scalars[ITERS + i, 0] * powers[1 + i]]
where the time goes in v2:
time: 54.8 us; the launch traced here: 54.4 us
  Pallas kernels  42.5 us (78%)
  local copies, waits for them, and re-layouts  6.1 us (11%)
  other arithmetic  4.45 us (8%)
  between operations  1.3 us (2%)
    pallas_call x1, Pallas kernels, body(): pl.pallas_call(functools.partial(kernel, ny, nz, nx), out_shape=(jax.Shap...  42.5 us
    unnamed x14, local copies, waits for them, and re-layouts  5.5 us
    unnamed x1, other arithmetic  4.45 us

profile of v2, /device:TPU:1, one launch (start us, length us, event | category | flops | bytes accessed | tf_op | source)
XLA Modules:
  0.0 54.4 jit_solution(13847794654414450054)
XLA Ops:
  1.3 0.0 copy-start
  1.3 0.9 %copy-done = f32[2,1,8,2048]{3,2,1,0:T(8,128)S(1)} copy-done((f32[2,1,8,2048]{3,2,1,0:T(8,128)S(1)}, f32[2,1,8,2048]{3,2,1,0:T(8,128)}, u32[]{:S(2)}) %copy-start) | copy-done | bytes 131096
  2.2 0.0 copy-start.1
  2.2 0.8 %copy-done.1 = f32[1,8,2048]{2,1,0:T(8,128)S(1)} copy-done((f32[1,8,2048]{2,1,0:T(8,128)S(1)}, f32[1,8,2048]{2,1,0:T(8,128)}, u32[]{:S(2)}) %copy-start.1) | copy-done | bytes 65560
  3.0 0.0 copy-start.2
  3.0 0.8 %copy-done.2 = f32[1,8,2048]{2,1,0:T(8,128)S(1)} copy-done((f32[1,8,2048]{2,1,0:T(8,128)S(1)}, f32[1,8,2048]{2,1,0:T(8,128)}, u32[]{:S(2)}) %copy-start.2) | copy-done | bytes 65560
  3.9 0.0 copy-start.3
  3.9 0.8 %copy-done.3 = f32[1,8,2048]{2,1,0:T(8,128)S(1)} copy-done((f32[1,8,2048]{2,1,0:T(8,128)S(1)}, f32[1,8,2048]{2,1,0:T(8,128)}, u32[]{:S(2)}) %copy-start.3) | copy-done | bytes 65560
  4.7 0.0 copy-start.4
  4.7 0.7 %copy-done.4 = f32[4,1,1,1024]{3,2,1,0:T(1,128)S(1)} copy-done((f32[4,1,1,1024]{3,2,1,0:T(1,128)S(1)}, f32[4,1,1,1024]{3,2,1,0:T(1,128)}, u32[]{:S(2)}) %copy-start.4) | copy-done | bytes 16408
  5.4 0.0 copy-start.5
  5.4 0.7 %copy-done.5 = s32[1,1,1024]{2,1,0:T(1,128)S(1)} copy-done((s32[1,1,1024]{2,1,0:T(1,128)S(1)}, s32[1,1,1024]{2,1,0:T(1,128)}, u32[]{:S(2)}) %copy-start.5) | copy-done | bytes 4120
  6.1 0.0 copy-start.6
  6.1 0.7 %copy-done.6 = s32[1,1,1024]{2,1,0:T(1,128)S(1)} copy-done((s32[1,1,1024]{2,1,0:T(1,128)S(1)}, s32[1,1,1024]{2,1,0:T(1,128)}, u32[]{:S(2)}) %copy-start.6) | copy-done | bytes 4120
  6.8 42.5 %shard_map.95 = (f32[3,2,8,2048]{3,2,1,0:T(8,128)S(1)}, f32[8,128]{1,0:T(8,128)S(1)}) custom-call(f32[2,1,8,2048]{3,2,1,0:T(8,128)S(1)} %copy-done, f32[1,8,2048]{2,1,0:T(8,128)S(1)} %copy-done.1, f32[1,8,2048]{2,1,0:T(8,128)S(1)} %copy-done.2, f32[1,8,2048]{2,1,0:T(8,128)S(1)} %copy-done.3, s32[1,1,1024]{2,1,0:T(1,128)S(1)} %copy-done.5, ...), custom_call_target="tpu_custom_call" | custom-call | tf_op jit(solution)/shard_map/pallas_call | solution.py:424
  49.3 0.6 %fusion.2 = (f32[1,1]{1,0:T(1,128)}, f32[1,1]{1,0:T(1,128)}, f32[1,1]{1,0:T(1,128)}, f32[1,1]{1,0:T(1,128)}, f32[1,1]{1,0:T(1,128)}, /*index=5*/f32[1,1]{1,0:T(1,128)}) fusion(f32[8,128]{1,0:T(8,128)S(1)} %get-tuple-element.4), kind=kLoop, calls=%fused_computation.6 | loop fusion | bytes 48 | tf_op jit(solution)/shard_map/slice | solution.py:466
  49.9 4.5 %fusion = (f32[2,1,8,2048]{3,2,1,0:T(8,128)}, f32[2,1,8,2048]{3,2,1,0:T(8,128)}) fusion(f32[2,1,8,2048]{3,2,1,0:T(8,128)S(1)} %copy-done, f32[3,2,8,2048]{3,2,1,0:T(8,128)S(1)} %get-tuple-element.5, f32[]{:T(128)} %bitcast.9, f32[]{:T(128)} %bitcast.8, f32[]{:T(128)} %bitcast.7, f32[]{:T(128)} %bitcast.4, f32[]{:T(128)} %bitcast.2, f32[]{:T(128)} %bitcast), kind=kLoop, calls=%fused_computation.1 | loop fusion | flops 360448 | bytes 786456
Async XLA Ops:
  1.3 0.9 %copy-start = (f32[2,1,8,2048]{3,2,1,0:T(8,128)S(1)}, f32[2,1,8,2048]{3,2,1,0:T(8,128)}, u32[]{:S(2)}) copy-start(f32[2,1,8,2048]{3,2,1,0:T(8,128)} %rhs_hbm.1) | copy-start | bytes 393220
  2.2 0.8 %copy-start.1 = (f32[1,8,2048]{2,1,0:T(8,128)S(1)}, f32[1,8,2048]{2,1,0:T(8,128)}, u32[]{:S(2)}) copy-start(f32[1,8,2048]{2,1,0:T(8,128)} %across_hbm.1) | copy-start | bytes 196612
  3.0 0.8 %copy-start.2 = (f32[1,8,2048]{2,1,0:T(8,128)S(1)}, f32[1,8,2048]{2,1,0:T(8,128)}, u32[]{:S(2)}) copy-start(f32[1,8,2048]{2,1,0:T(8,128)} %down_hbm.1) | copy-start | bytes 196612
  3.9 0.8 %copy-start.3 = (f32[1,8,2048]{2,1,0:T(8,128)S(1)}, f32[1,8,2048]{2,1,0:T(8,128)}, u32[]{:S(2)}) copy-start(f32[1,8,2048]{2,1,0:T(8,128)} %anchor_hbm.1) | copy-start | bytes 196612
  4.7 0.7 %copy-start.4 = (f32[4,1,1,1024]{3,2,1,0:T(1,128)S(1)}, f32[4,1,1,1024]{3,2,1,0:T(1,128)}, u32[]{:S(2)}) copy-start(f32[4,1,1,1024]{3,2,1,0:T(1,128)} %weight_hbm.1) | copy-start | bytes 49156
  5.4 0.7 %copy-start.5 = (s32[1,1,1024]{2,1,0:T(1,128)S(1)}, s32[1,1,1024]{2,1,0:T(1,128)}, u32[]{:S(2)}) copy-start(s32[1,1,1024]{2,1,0:T(1,128)} %source_hbm.1) | copy-start | bytes 12292
  6.1 0.7 %copy-start.6 = (s32[1,1,1024]{2,1,0:T(1,128)S(1)}, s32[1,1,1024]{2,1,0:T(1,128)}, u32[]{:S(2)}) copy-start(s32[1,1,1024]{2,1,0:T(1,128)} %target_hbm.1) | copy-start | bytes 12292

commit v3 on v2

--- a/solution.py
+++ b/solution.py
@@ -124,8 +124,8 @@
     target_hbm,
     weight_hbm,
     count_hbm,
-    basis,
-    scalars,
+    x_ref,
+    r_ref,
     rhs_ref,
     across_ref,
     down_ref,
@@ -138,6 +138,7 @@
     mask_source,
     mask_left,
     mask_right,
+    basis,
     weight_out,
     rim_out,
     halo_out,
@@ -395,11 +396,10 @@
         jnp.sum(jnp.where(lane == i, total, 0.0), 1, keepdims=True) for i in range(MOMENTS)
     ]
     steps, rest = coefficients(mu)
-    scalars[...] = jnp.concatenate(
-        [jnp.broadcast_to(s, (1, 128)) for s in [s * (1.0 / SCALE) for s in steps] + rest[1:]]
-        + [jnp.zeros((8 - 2 * ITERS, 128), jnp.float32)],
-        0,
-    )
+    for c in range(2):
+        powers = [rhs_ref[c, 0]] + [basis[i, c] for i in range(ITERS)]
+        x_ref[c, 0] = sum((s * (1.0 / SCALE)) * v for s, v in zip(steps, powers))
+        r_ref[c, 0] = sum((v if s is None else s * v) for s, v in zip(rest, powers))
 
     for copy in sent:
         copy.wait_send()
@@ -421,12 +421,10 @@
     args = (rhs, across, down, anchor, source, target, weight, count)
     copies = 3 + 4 * ITERS + 2
     widest = max(nx * ny, nz)
-    basis, scalars = pl.pallas_call(
+    out = jax.ShapeDtypeStruct(rhs.shape, f32)
+    return pl.pallas_call(
         functools.partial(kernel, ny, nz, nx),
-        out_shape=(
-            jax.ShapeDtypeStruct((ITERS, 2, rows, cols), f32),
-            jax.ShapeDtypeStruct((8, 128), f32),
-        ),
+        out_shape=(out, out),
         in_specs=[hbm] * len(args),
         out_specs=(vmem, vmem),
         scratch_shapes=[
@@ -442,6 +440,7 @@
             pltpu.VMEM((places, slots), f32),
             pltpu.VMEM((places, slots), f32),
             pltpu.VMEM((places, slots), f32),
+            pltpu.VMEM((ITERS, 2, rows, cols), f32),
             pltpu.VMEM((4, 1, slots), f32),
             pltpu.VMEM((1, cols), f32),
             pltpu.VMEM((ITERS, 2, 2, cols), f32),
@@ -458,13 +457,9 @@
             pltpu.SemaphoreType.REGULAR((3,)),
         ],
         compiler_params=pltpu.CompilerParams(
-            collective_id=0, has_side_effects=True, vmem_limit_bytes=48 * 1024 * 1024
+            collective_id=0, has_side_effects=True, vmem_limit_bytes=63 * 1024 * 1024
         ),
     )(*args)
-    powers = [rhs[:, 0]] + [basis[i] for i in range(ITERS)]
-    field = sum(scalars[i, 0] * powers[i] for i in range(ITERS))
-    residual = powers[0] + sum(scalars[ITERS + i, 0] * powers[1 + i] for i in range(ITERS))
-    return field[:, None], residual[:, None]
 
 
 def solution(mesh, nz=16):

time: 54.8 us -> 47.1 us (0.86)
  other arithmetic: 4.45 us -> 0 us
  local copies, waits for them, and re-layouts: 6.1 us -> 2.26 us
  Pallas kernels: 42.5 us -> 43.4 us
    unnamed x1 -> x0, other arithmetic: 4.45 us -> none
    unnamed x14 -> x4, local copies, waits for them, and re-layouts: 5.5 us -> 2.26 us
    pallas_call x1, Pallas kernels: 42.5 us -> 43.4 us  [body(): pl.pallas_call(functools.partial(kernel, ny, nz, nx), out_shape=(out, out...]
    slice x1 -> x0, local copies, waits for them, and re-layouts: 0.6 us -> none  [body(): scalars[ITERS + i, 0] * powers[1 + i]]
where the time goes in v3:
time: 47.1 us; the launch traced here: 47 us
  Pallas kernels  43.4 us (92%)
  local copies, waits for them, and re-layouts  2.26 us (5%)
  between operations  1.3 us (3%)
    pallas_call x1, Pallas kernels, body(): pl.pallas_call(functools.partial(kernel, ny, nz, nx), out_shape=(out, out...  43.4 us
    unnamed x4, local copies, waits for them, and re-layouts  2.26 us

profile of v3, /device:TPU:1, one launch (start us, length us, event | category | flops | bytes accessed | tf_op | source)
XLA Modules:
  0.0 47.0 jit_solution(15231929476353405689)
XLA Ops:
  1.3 43.4 %shard_map.95 = (f32[2,1,8,2048]{3,2,1,0:T(8,128)}, f32[2,1,8,2048]{3,2,1,0:T(8,128)}) custom-call(f32[2,1,8,2048]{3,2,1,0:T(8,128)} %rhs_hbm.1, f32[1,8,2048]{2,1,0:T(8,128)} %across_hbm.1, f32[1,8,2048]{2,1,0:T(8,128)} %down_hbm.1, f32[1,8,2048]{2,1,0:T(8,128)} %anchor_hbm.1, s32[1,1,1024]{2,1,0:T(1,128)} %source_hbm.1, s32[1,1,1024]{2,1,0:T(1,128)} %target_hbm.1, ...), custom_call_target="tpu_custom_call" | custom-call | tf_op jit(solution)/shard_map/pallas_call | solution.py:425
  44.7 0.0 copy-start
  44.7 1.6 %copy.13 = f32[2,1,8,2048]{3,2,1,0:T(8,128)} copy(f32[2,1,8,2048]{3,2,1,0:T(8,128)} %get-tuple-element.4) | data formatting | bytes 262144
  46.3 0.0 copy-done
  46.3 0.7 %copy.14 = f32[2,1,8,2048]{3,2,1,0:T(8,128)} copy(f32[2,1,8,2048]{3,2,1,0:T(8,128)S(1)} %copy-done) | data formatting | bytes 262144
Async XLA Ops:
  44.7 1.6 %copy-start = (f32[2,1,8,2048]{3,2,1,0:T(8,128)S(1)}, f32[2,1,8,2048]{3,2,1,0:T(8,128)}, u32[]{:S(2)}) copy-start(f32[2,1,8,2048]{3,2,1,0:T(8,128)} %get-tuple-element.5) | copy-start | bytes 393220

commit v4 on v2

--- a/solution.py
+++ b/solution.py
@@ -124,7 +124,7 @@
     target_hbm,
     weight_hbm,
     count_hbm,
-    basis,
+    basis_hbm,
     scalars,
     rhs_ref,
     across_ref,
@@ -138,6 +138,7 @@
     mask_source,
     mask_left,
     mask_right,
+    basis,
     weight_out,
     rim_out,
     halo_out,
@@ -151,6 +152,7 @@
     send_sem,
     recv_sem,
     load_sem,
+    keep_sem,
     greet_sem,
 ):
     rows, cols = across_ref.shape[1:]
@@ -211,7 +213,7 @@
     for load in loads:
         load.start()
 
-    sent = []
+    sent, kept = [], []
 
     def send(src, dst, peer, index):
         copy = pltpu.make_async_remote_copy(
@@ -386,6 +388,9 @@
             products.append(sum(folded(a * a) for a in latest))
         for c in range(2):
             basis[k, c] = latest[c]
+        keep = pltpu.make_async_copy(basis.at[k], basis_hbm.at[k], keep_sem.at[k])
+        keep.start()
+        kept.append(keep)
         field = latest
 
     post_sum(1, take_sum(0))
@@ -395,18 +400,40 @@
         jnp.sum(jnp.where(lane == i, total, 0.0), 1, keepdims=True) for i in range(MOMENTS)
     ]
     steps, rest = coefficients(mu)
-    scalars[...] = jnp.concatenate(
-        [jnp.broadcast_to(s, (1, 128)) for s in [s * (1.0 / SCALE) for s in steps] + rest[1:]]
-        + [jnp.zeros((8 - 2 * ITERS, 128), jnp.float32)],
-        0,
-    )
-
+    rows_of = [jnp.broadcast_to(s, (1, 128)) for s in [s * (1.0 / SCALE) for s in steps] + rest[1:]]
+    scalars[...] = jnp.concatenate(rows_of + [jnp.zeros((8 - 2 * ITERS, 128), jnp.float32)], 0)
+
+    for keep in kept:
+        keep.wait()
     for copy in sent:
         copy.wait_send()
     for stage in range(2):
         count = len(groups[stage])
         gone = sums.at[stage, pl.ds(1, count)]
         pltpu.make_async_copy(gone, gone, send_sem.at[3 + 4 * ITERS + stage]).wait()
+
+
+def combine(rhs_hbm, basis_hbm, scalars_hbm, x_hbm, r_hbm, rhs, basis, scalars, x, r, load_sem, save_sem):
+    loads = [
+        pltpu.make_async_copy(src, dst, load_sem.at[i])
+        for i, (src, dst) in enumerate(((scalars_hbm, scalars), (rhs_hbm, rhs), (basis_hbm, basis)))
+    ]
+    for load in loads:
+        load.start()
+    for load in loads:
+        load.wait()
+    values = [scalars[i : i + 1, :1] for i in range(2 * ITERS)]
+    saves = []
+    for c in range(2):
+        powers = [rhs[c, 0]] + [basis[i, c] for i in range(ITERS)]
+        x[c, 0] = sum(s * v for s, v in zip(values[:ITERS], powers))
+        r[c, 0] = powers[0] + sum(s * v for s, v in zip(values[ITERS:], powers[1:]))
+        for n, (src, dst) in enumerate(((x, x_hbm), (r, r_hbm))):
+            save = pltpu.make_async_copy(src.at[c], dst.at[c], save_sem.at[2 * c + n])
+            save.start()
+            saves.append(save)
+    for save in saves:
+        save.wait()
 
 
 def body(nz, rhs, across, down, anchor, source, target, weight, count):
@@ -428,7 +455,7 @@
             jax.ShapeDtypeStruct((8, 128), f32),
         ),
         in_specs=[hbm] * len(args),
-        out_specs=(vmem, vmem),
+        out_specs=(hbm, vmem),
         scratch_shapes=[
             pltpu.VMEM(rhs.shape, f32),
             pltpu.VMEM(across.shape, f32),
@@ -442,6 +469,7 @@
             pltpu.VMEM((places, slots), f32),
             pltpu.VMEM((places, slots), f32),
             pltpu.VMEM((places, slots), f32),
+            pltpu.VMEM((ITERS, 2, rows, cols), f32),
             pltpu.VMEM((4, 1, slots), f32),
             pltpu.VMEM((1, cols), f32),
             pltpu.VMEM((ITERS, 2, 2, cols), f32),
@@ -455,16 +483,30 @@
             pltpu.SemaphoreType.DMA((copies,)),
             pltpu.SemaphoreType.DMA((copies,)),
             pltpu.SemaphoreType.DMA((7,)),
+            pltpu.SemaphoreType.DMA((ITERS,)),
             pltpu.SemaphoreType.REGULAR((3,)),
         ],
         compiler_params=pltpu.CompilerParams(
-            collective_id=0, has_side_effects=True, vmem_limit_bytes=48 * 1024 * 1024
+            collective_id=0, has_side_effects=True, vmem_limit_bytes=63 * 1024 * 1024
         ),
     )(*args)
-    powers = [rhs[:, 0]] + [basis[i] for i in range(ITERS)]
-    field = sum(scalars[i, 0] * powers[i] for i in range(ITERS))
-    residual = powers[0] + sum(scalars[ITERS + i, 0] * powers[1 + i] for i in range(ITERS))
-    return field[:, None], residual[:, None]
+    out = jax.ShapeDtypeStruct(rhs.shape, f32)
+    return pl.pallas_call(
+        combine,
+        out_shape=(out, out),
+        in_specs=[hbm] * 3,
+        out_specs=(hbm, hbm),
+        scratch_shapes=[
+            pltpu.VMEM(rhs.shape, f32),
+            pltpu.VMEM(basis.shape, f32),
+            pltpu.VMEM(scalars.shape, f32),
+            pltpu.VMEM(rhs.shape, f32),
+            pltpu.VMEM(rhs.shape, f32),
+            pltpu.SemaphoreType.DMA((3,)),
+            pltpu.SemaphoreType.DMA((4,)),
+        ],
+        compiler_params=pltpu.CompilerParams(vmem_limit_bytes=63 * 1024 * 1024),
+    )(rhs, basis, scalars)
 
 
 def solution(mesh, nz=16):

time: 54.8 us -> 46.7 us (0.85)
  local copies, waits for them, and re-layouts: 6.1 us -> 0 us
  other arithmetic: 4.45 us -> 0 us
  Pallas kernels: 42.5 us -> 45.1 us
    unnamed x14 -> x0, local copies, waits for them, and re-layouts: 5.5 us -> none
    unnamed x1 -> x0, other arithmetic: 4.45 us -> none
    pallas_call x0 -> x1, Pallas kernels: none -> 1.87 us  [body(): pl.pallas_call(combine, out_shape=(out, out), in_specs=[hbm] * 3, out_spe...]
    pallas_call x1, Pallas kernels: 42.5 us -> 43.3 us  [body(): pl.pallas_call(functools.partial(kernel, ny, nz, nx), out_shape=(jax.Shap...]
    slice x1 -> x0, local copies, waits for them, and re-layouts: 0.6 us -> none  [body(): scalars[ITERS + i, 0] * powers[1 + i]]
where the time goes in v4:
time: 46.7 us; the launch traced here: 46.4 us
  Pallas kernels  45.1 us (97%)
  between operations  1.29 us (3%)
    pallas_call x1, Pallas kernels, body(): pl.pallas_call(functools.partial(kernel, ny, nz, nx), out_shape=(jax.Shap...  43.3 us
    pallas_call x1, Pallas kernels, body(): pl.pallas_call(combine, out_shape=(out, out), in_specs=[hbm] * 3, out_spe...  1.87 us

profile of v4, /device:TPU:1, one launch (start us, length us, event | category | flops | bytes accessed | tf_op | source)
XLA Modules:
  0.0 46.4 jit_solution(1851381745155064424)
XLA Ops:
  1.3 43.3 %shard_map.95 = (f32[3,2,8,2048]{3,2,1,0:T(8,128)}, f32[8,128]{1,0:T(8,128)}) custom-call(f32[2,1,8,2048]{3,2,1,0:T(8,128)} %rhs_hbm.3, f32[1,8,2048]{2,1,0:T(8,128)} %across_hbm.1, f32[1,8,2048]{2,1,0:T(8,128)} %down_hbm.1, f32[1,8,2048]{2,1,0:T(8,128)} %anchor_hbm.1, s32[1,1,1024]{2,1,0:T(1,128)} %source_hbm.1, s32[1,1,1024]{2,1,0:T(1,128)} %target_hbm.1, ...), custom_call_target="tpu_custom_call" | custom-call | tf_op jit(solution)/shard_map/pallas_call | solution.py:451
  44.5 1.9 %shard_map.96 = (f32[2,1,8,2048]{3,2,1,0:T(8,128)}, f32[2,1,8,2048]{3,2,1,0:T(8,128)}) custom-call(f32[2,1,8,2048]{3,2,1,0:T(8,128)} %rhs_hbm.3, f32[3,2,8,2048]{3,2,1,0:T(8,128)} %get-tuple-element.4.basis_hbm, f32[8,128]{1,0:T(8,128)} %get-tuple-element.5.scalars_hbm), custom_call_target="tpu_custom_call" | custom-call | tf_op jit(solution)/shard_map/pallas_call | solution.py:494

commit v5 on v4

--- a/solution.py
+++ b/solution.py
@@ -131,6 +131,7 @@
     down_ref,
     anchor_ref,
     source_ref,
+    target_ref,
     weight_ref,
     count_ref,
     hot_source,
@@ -139,12 +140,11 @@
     mask_left,
     mask_right,
     basis,
-    weight_out,
+    slot_out,
     rim_out,
     halo_out,
     point_out,
-    target_in,
-    weight_in,
+    slot_in,
     rim_in,
     halo_in,
     point_in,
@@ -207,6 +207,7 @@
                 (down_hbm, down_ref),
                 (across_hbm, across_ref),
                 (anchor_hbm, anchor_ref),
+                (target_hbm, target_ref),
             ]
         )
     ]
@@ -233,20 +234,21 @@
     loads[1].wait()
     live = ((slot < count_ref[0, 0] * BLOCK) & (gz < n_gz - 1)).astype(jnp.float32)
     for k in range(4):
-        weight_out[k] = weight_ref[k, 0] * live
+        slot_out[k] = weight_ref[k, 0] * live
+    loads[7].wait()
+    slot_out[4] = target_ref[0].astype(jnp.float32)
     def post_halo(field, k):
         for c in range(2):
             halo_out[k, 0, c : c + 1, :] = field[c][:1]
             halo_out[k, 1, c : c + 1, :] = field[c][rows - 1 :]
         return [
-            send(halo_out.at[k, 0], halo_in.at[k, 0], above, 3 + 4 * k),
-            send(halo_out.at[k, 1], halo_in.at[k, 1], below, 4 + 4 * k),
+            send(halo_out.at[k, 0], halo_in.at[k, 0], above, 2 + 4 * k),
+            send(halo_out.at[k, 1], halo_in.at[k, 1], below, 3 + 4 * k),
         ]
 
     pl.semaphore_wait(barrier, len(met))
     copies = [
-        send(target_hbm, target_in, after, 0),
-        send(weight_out, weight_in, after, 1),
+        send(slot_out, slot_in, after, 0),
     ]
     greet(0, one_hop)
 
@@ -255,7 +257,7 @@
     halo = post_halo(field, 0)
     loads[4].wait()
     rim_out[...] = down_ref[0, rows - 1 :]
-    copies.append(send(rim_out, rim_in, below, 2))
+    copies.append(send(rim_out, rim_in, below, 1))
 
     low_id = lax.broadcasted_iota(jnp.int32, (LOW, slots), 0)
     place_id = lax.broadcasted_iota(jnp.int32, (highs * rows, slots), 0)
@@ -275,10 +277,10 @@
     across, down, anchor = across_ref[0], down_ref[0], anchor_ref[0]
     col_id = lax.broadcasted_iota(jnp.int32, (rows, cols), 1)
     row_id = lax.broadcasted_iota(jnp.int32, (rows, cols), 0)
-    products = [sum(folded(f * f) for f in field)]
+    products = []
 
     for k in range(ITERS):
-        base = 3 + 4 * k
+        base = 2 + 4 * k
         own = looked_up(pieces(stacked(field), 3), hot_source, [mask_source], 3)
         for c in range(2):
             point_out[k, 0, c : c + 1, :] = own[c]
@@ -286,14 +288,13 @@
         right = [jnp.where(col_id == cols - 1, 0.0, pltpu.roll(f, cols - 1, 1)) for f in field]
         if k == 0:
             copies[0].wait_recv()
-            copies[1].wait_recv()
-            low, place = split(target_in[0])
+            low, place = split(slot_in[4].astype(jnp.int32))
             hot_target[...] = (low_id == low).astype(jnp.float32).astype(jnp.bfloat16)
             for mask, one, two in ((mask_left, 0, 2), (mask_right, 1, 3)):
                 mask[...] = jnp.where(
                     place_id == place,
-                    weight_in[one],
-                    jnp.where(place_id == place + 1, weight_in[two], 0.0),
+                    slot_in[one],
+                    jnp.where(place_id == place + 1, slot_in[two], 0.0),
                 )
         table = jnp.concatenate([pieces(stacked(field), 3), pieces(stacked(right), 3)], 0)
         there = looked_up(table, hot_target, [mask_left, mask_right], 3)
@@ -301,55 +302,69 @@
             point_out[k, 1, c : c + 1, :] = there[c]
         there_copy = send(point_out.at[k, 1], point_in.at[k, 1], before, base + 3)
 
-        if k == 0:
-            copies[2].wait_recv()
-        halo[0].wait_recv()
-        halo[1].wait_recv()
         image, energy = [], None
         for c in range(2):
             f = field[c]
-            upper = jnp.where(xy > 0, halo_in[k, 1, c : c + 1, :], 0.0)
-            lower = jnp.where(xy < nx - 1, halo_in[k, 0, c : c + 1, :], 0.0)
-            rim = jnp.where(xy > 0, rim_in[...], 0.0)
             gap = f - right[c]
             flux = across * gap
-            fall = f - jnp.where(row_id == rows - 1, lower, pltpu.roll(f, rows - 1, 0))
+            fall = jnp.where(row_id == rows - 1, 0.0, f - pltpu.roll(f, rows - 1, 0))
             drop = down * fall
             held = anchor * f
             come = jnp.where(col_id == 0, 0.0, pltpu.roll(flux, 1, 1))
-            down_in = jnp.where(row_id == 0, rim * (upper - f), pltpu.roll(drop, 1, 0))
-            image.append(flux - come + drop - down_in + held)
+            above_me = jnp.where(row_id == 0, 0.0, pltpu.roll(drop, 1, 0))
+            image.append(flux - come + drop - above_me + held)
             if k == ITERS - 1:
                 term = flux * gap + drop * fall + held * f
                 energy = term if energy is None else energy + term
-
-        own_copy.wait_recv()
+        if k > 0:
+            products.append(sum(folded(a * b) for a, b in zip(former, field)))
+        products.append(sum(folded(a * a) for a in field))
+        if k == ITERS - 1:
+            rows_known = [jnp.sum(p, 0, keepdims=True) for p in products]
+            energy = folded(energy)
+
         if k == 0:
             pl.semaphore_wait(greet_sem.at[0], len(one_hop))
             greet(1, two_hops)
         if k == 1:
             pl.semaphore_wait(greet_sem.at[1], len(two_hops))
             greet(2, four_hops)
-        error_in = [there[c] - point_in[k, 0, c : c + 1, :] for c in range(2)]
 
         def onward():
+            own_copy.wait_recv()
+            error_in = [there[c] - point_in[k, 0, c : c + 1, :] for c in range(2)]
             left = unstacked(spread(error_in, mask_left, hot_target, 2), rows, highs)
             more = unstacked(spread(error_in, mask_right, hot_target, 2), rows, highs)
             return [a + pltpu.roll(b, 1, 1) for a, b in zip(left, more)]
 
         if k < ITERS - 1:
             image = [a + b for a, b in zip(image, onward())]
+
+        if k == 0:
+            copies[1].wait_recv()
+        halo[0].wait_recv()
+        halo[1].wait_recv()
+        rim = jnp.where(xy > 0, rim_in[...], 0.0)
+        for c in range(2):
+            f = field[c]
+            upper = halo_in[k, 1, c : c + 1, :]
+            lower = jnp.where(xy < nx - 1, halo_in[k, 0, c : c + 1, :], 0.0)
+            fall = f - lower
+            drop = down * fall
+            edge = jnp.where(row_id == 0, rim * (f - upper), 0.0)
+            image[c] = image[c] + jnp.where(row_id == rows - 1, drop + edge, edge)
+            if k == ITERS - 1:
+                energy = energy + folded(jnp.where(row_id == rows - 1, drop * fall, 0.0))
+
         there_copy.wait_recv()
         error = [point_in[k, 1, c : c + 1, :] - own[c] for c in range(2)]
         if k == ITERS - 1:
             tie = sum(e * e for e in error)
-            last = folded(energy) * (1.0 / SCALE)
-            last_tie = folded(tie) * (1.0 / SCALE)
-            products.append(last)
-            lanes = jnp.concatenate([jnp.sum(p, 0, keepdims=True) for p in products], 0)
-            lanes = jnp.concatenate([lanes, jnp.zeros((8 - MOMENTS, 128), jnp.float32)], 0)
+            last = jnp.sum(energy, 0, keepdims=True) + folded(tie)
+            rows_known.append(last * (1.0 / SCALE))
+            rows_known.append(jnp.zeros((8 - MOMENTS, 128), jnp.float32))
+            lanes = jnp.concatenate(rows_known, 0)
             eight = lax.broadcasted_iota(jnp.int32, (8, 128), 0)
-            lanes = lanes + jnp.where(eight == MOMENTS - 1, last_tie, 0.0)
             total = jnp.sum(lanes, 1, keepdims=True)
             lane = lax.broadcasted_iota(jnp.int32, (8, 128), 1)
             total = jnp.sum(jnp.where(lane == eight, total, 0.0), 0, keepdims=True)
@@ -358,7 +373,7 @@
             sums[stage, 0] = total
             if stage == 0:
                 pl.semaphore_wait(greet_sem.at[2], len(four_hops))
-            index = 3 + 4 * ITERS + stage
+            index = 2 + 4 * ITERS + stage
             for i, peer in enumerate(groups[stage]):
                 copy = pltpu.make_async_remote_copy(
                     src_ref=sums.at[stage, 0],
@@ -371,7 +386,7 @@
                 copy.start()
 
         def take_sum(stage):
-            index = 3 + 4 * ITERS + stage
+            index = 2 + 4 * ITERS + stage
             count = len(groups[stage])
             arrived = sums.at[stage, pl.ds(1, count)]
             pltpu.make_async_copy(arrived, arrived, recv_sem.at[index]).wait()
@@ -384,14 +399,12 @@
         latest = [(a - b) * (1.0 / SCALE) for a, b in zip(image, back)]
         if k < ITERS - 1:
             halo = post_halo(latest, k + 1)
-            products.append(sum(folded(a * b) for a, b in zip(field, latest)))
-            products.append(sum(folded(a * a) for a in latest))
         for c in range(2):
             basis[k, c] = latest[c]
         keep = pltpu.make_async_copy(basis.at[k], basis_hbm.at[k], keep_sem.at[k])
         keep.start()
         kept.append(keep)
-        field = latest
+        former, field = field, latest
 
     post_sum(1, take_sum(0))
     total = take_sum(1)
@@ -410,7 +423,7 @@
     for stage in range(2):
         count = len(groups[stage])
         gone = sums.at[stage, pl.ds(1, count)]
-        pltpu.make_async_copy(gone, gone, send_sem.at[3 + 4 * ITERS + stage]).wait()
+        pltpu.make_async_copy(gone, gone, send_sem.at[2 + 4 * ITERS + stage]).wait()
 
 
 def combine(rhs_hbm, basis_hbm, scalars_hbm, x_hbm, r_hbm, rhs, basis, scalars, x, r, load_sem, save_sem):
@@ -446,7 +459,7 @@
     vmem = pl.BlockSpec(memory_space=pltpu.VMEM)
     hbm = pl.BlockSpec(memory_space=pltpu.HBM)
     args = (rhs, across, down, anchor, source, target, weight, count)
-    copies = 3 + 4 * ITERS + 2
+    copies = 2 + 4 * ITERS + 2
     widest = max(nx * ny, nz)
     basis, scalars = pl.pallas_call(
         functools.partial(kernel, ny, nz, nx),
@@ -462,6 +475,7 @@
             pltpu.VMEM(down.shape, f32),
             pltpu.VMEM(anchor.shape, f32),
             pltpu.VMEM(source.shape, jnp.int32),
+            pltpu.VMEM(target.shape, jnp.int32),
             pltpu.VMEM(weight.shape, f32),
             pltpu.SMEM(count.shape, jnp.int32),
             pltpu.VMEM((LOW, slots), bf16),
@@ -470,19 +484,18 @@
             pltpu.VMEM((places, slots), f32),
             pltpu.VMEM((places, slots), f32),
             pltpu.VMEM((ITERS, 2, rows, cols), f32),
-            pltpu.VMEM((4, 1, slots), f32),
+            pltpu.VMEM((5, 1, slots), f32),
             pltpu.VMEM((1, cols), f32),
             pltpu.VMEM((ITERS, 2, 2, cols), f32),
             pltpu.VMEM((ITERS, 2, 2, slots), f32),
-            pltpu.VMEM((1, 1, slots), jnp.int32),
-            pltpu.VMEM((4, 1, slots), f32),
+            pltpu.VMEM((5, 1, slots), f32),
             pltpu.VMEM((1, cols), f32),
             pltpu.VMEM((ITERS, 2, 2, cols), f32),
             pltpu.VMEM((ITERS, 2, 2, slots), f32),
             pltpu.VMEM((2, widest, 1, 128), f32),
             pltpu.SemaphoreType.DMA((copies,)),
             pltpu.SemaphoreType.DMA((copies,)),
-            pltpu.SemaphoreType.DMA((7,)),
+            pltpu.SemaphoreType.DMA((8,)),
             pltpu.SemaphoreType.DMA((ITERS,)),
             pltpu.SemaphoreType.REGULAR((3,)),
         ],

time: 46.7 us -> 46.2 us (0.989)
  Pallas kernels: 45.1 us -> 44.6 us
    pallas_call x1, Pallas kernels: 43.3 us -> 42.7 us  [body(): pl.pallas_call(functools.partial(kernel, ny, nz, nx), out_shape=(jax.Shap...]
where the time goes in v5:
time: 46.2 us; the launch traced here: 45.9 us
  Pallas kernels  44.6 us (97%)
  between operations  1.29 us (3%)
    pallas_call x1, Pallas kernels, body(): pl.pallas_call(functools.partial(kernel, ny, nz, nx), out_shape=(jax.Shap...  42.7 us
    pallas_call x1, Pallas kernels, body(): pl.pallas_call(combine, out_shape=(out, out), in_specs=[hbm] * 3, out_spe...  1.87 us

profile of v5, /device:TPU:1, one launch (start us, length us, event | category | flops | bytes accessed | tf_op | source)
XLA Modules:
  0.0 45.9 jit_solution(15815435729654141248)
XLA Ops:
  1.3 42.7 %shard_map.95 = (f32[3,2,8,2048]{3,2,1,0:T(8,128)}, f32[8,128]{1,0:T(8,128)}) custom-call(f32[2,1,8,2048]{3,2,1,0:T(8,128)} %rhs_hbm.3, f32[1,8,2048]{2,1,0:T(8,128)} %across_hbm.1, f32[1,8,2048]{2,1,0:T(8,128)} %down_hbm.1, f32[1,8,2048]{2,1,0:T(8,128)} %anchor_hbm.1, s32[1,1,1024]{2,1,0:T(1,128)} %source_hbm.1, s32[1,1,1024]{2,1,0:T(1,128)} %target_hbm.1, ...), custom_call_target="tpu_custom_call" | custom-call | tf_op jit(solution)/shard_map/pallas_call | solution.py:464
  44.0 1.9 %shard_map.96 = (f32[2,1,8,2048]{3,2,1,0:T(8,128)}, f32[2,1,8,2048]{3,2,1,0:T(8,128)}) custom-call(f32[2,1,8,2048]{3,2,1,0:T(8,128)} %rhs_hbm.3, f32[3,2,8,2048]{3,2,1,0:T(8,128)} %get-tuple-element.4.basis_hbm, f32[8,128]{1,0:T(8,128)} %get-tuple-element.5.scalars_hbm), custom_call_target="tpu_custom_call" | custom-call | tf_op jit(solution)/shard_map/pallas_call | solution.py:507

commit v6 on v5

--- a/solution.py
+++ b/solution.py
@@ -281,7 +281,7 @@
 
     for k in range(ITERS):
         base = 2 + 4 * k
-        own = looked_up(pieces(stacked(field), 3), hot_source, [mask_source], 3)
+        own = looked_up(pieces(stacked(field), 2), hot_source, [mask_source], 2)
         for c in range(2):
             point_out[k, 0, c : c + 1, :] = own[c]
         own_copy = send(point_out.at[k, 0], point_in.at[k, 0], after, base + 2)
@@ -296,8 +296,8 @@
                     slot_in[one],
                     jnp.where(place_id == place + 1, slot_in[two], 0.0),
                 )
-        table = jnp.concatenate([pieces(stacked(field), 3), pieces(stacked(right), 3)], 0)
-        there = looked_up(table, hot_target, [mask_left, mask_right], 3)
+        table = jnp.concatenate([pieces(stacked(field), 2), pieces(stacked(right), 2)], 0)
+        there = looked_up(table, hot_target, [mask_left, mask_right], 2)
         for c in range(2):
             point_out[k, 1, c : c + 1, :] = there[c]
         there_copy = send(point_out.at[k, 1], point_in.at[k, 1], before, base + 3)

time: 46.2 us -> 45.6 us (0.987)
  Pallas kernels: 44.6 us -> 44.1 us
    pallas_call x1, Pallas kernels: 42.7 us -> 42.2 us  [body(): pl.pallas_call(functools.partial(kernel, ny, nz, nx), out_shape=(jax.Shap...]
where the time goes in v6:
time: 45.6 us; the launch traced here: 45.3 us
  Pallas kernels  44.1 us (97%)
  between operations  1.29 us (3%)
    pallas_call x1, Pallas kernels, body(): pl.pallas_call(functools.partial(kernel, ny, nz, nx), out_shape=(jax.Shap...  42.2 us
    pallas_call x1, Pallas kernels, body(): pl.pallas_call(combine, out_shape=(out, out), in_specs=[hbm] * 3, out_spe...  1.87 us

profile of v6, /device:TPU:1, one launch (start us, length us, event | category | flops | bytes accessed | tf_op | source)
XLA Modules:
  0.0 45.3 jit_solution(17786645993734022485)
XLA Ops:
  1.3 42.2 %shard_map.95 = (f32[3,2,8,2048]{3,2,1,0:T(8,128)}, f32[8,128]{1,0:T(8,128)}) custom-call(f32[2,1,8,2048]{3,2,1,0:T(8,128)} %rhs_hbm.3, f32[1,8,2048]{2,1,0:T(8,128)} %across_hbm.1, f32[1,8,2048]{2,1,0:T(8,128)} %down_hbm.1, f32[1,8,2048]{2,1,0:T(8,128)} %anchor_hbm.1, s32[1,1,1024]{2,1,0:T(1,128)} %source_hbm.1, s32[1,1,1024]{2,1,0:T(1,128)} %target_hbm.1, ...), custom_call_target="tpu_custom_call" | custom-call | tf_op jit(solution)/shard_map/pallas_call | solution.py:464
  43.5 1.9 %shard_map.96 = (f32[2,1,8,2048]{3,2,1,0:T(8,128)}, f32[2,1,8,2048]{3,2,1,0:T(8,128)}) custom-call(f32[2,1,8,2048]{3,2,1,0:T(8,128)} %rhs_hbm.3, f32[3,2,8,2048]{3,2,1,0:T(8,128)} %get-tuple-element.4.basis_hbm, f32[8,128]{1,0:T(8,128)} %get-tuple-element.5.scalars_hbm), custom_call_target="tpu_custom_call" | custom-call | tf_op jit(solution)/shard_map/pallas_call | solution.py:507

commit v7 on v6

--- a/solution.py
+++ b/solution.py
@@ -285,6 +285,8 @@
         for c in range(2):
             point_out[k, 0, c : c + 1, :] = own[c]
         own_copy = send(point_out.at[k, 0], point_in.at[k, 0], after, base + 2)
+        if k > 0:
+            halo = post_halo(field, k)
         right = [jnp.where(col_id == cols - 1, 0.0, pltpu.roll(f, cols - 1, 1)) for f in field]
         if k == 0:
             copies[0].wait_recv()
@@ -397,8 +399,6 @@
             image = [a + b for a, b in zip(image, onward())]
         back = unstacked(spread(error, mask_source, hot_source, 2), rows, highs)
         latest = [(a - b) * (1.0 / SCALE) for a, b in zip(image, back)]
-        if k < ITERS - 1:
-            halo = post_halo(latest, k + 1)
         for c in range(2):
             basis[k, c] = latest[c]
         keep = pltpu.make_async_copy(basis.at[k], basis_hbm.at[k], keep_sem.at[k])
@@ -429,15 +429,23 @@
 def combine(rhs_hbm, basis_hbm, scalars_hbm, x_hbm, r_hbm, rhs, basis, scalars, x, r, load_sem, save_sem):
     loads = [
         pltpu.make_async_copy(src, dst, load_sem.at[i])
-        for i, (src, dst) in enumerate(((scalars_hbm, scalars), (rhs_hbm, rhs), (basis_hbm, basis)))
+        for i, (src, dst) in enumerate(
+            [(scalars_hbm, scalars)]
+            + [
+                pair
+                for c in range(2)
+                for pair in ((rhs_hbm.at[c], rhs.at[c]), (basis_hbm.at[:, c], basis.at[:, c]))
+            ]
+        )
     ]
     for load in loads:
         load.start()
-    for load in loads:
-        load.wait()
+    loads[0].wait()
     values = [scalars[i : i + 1, :1] for i in range(2 * ITERS)]
     saves = []
     for c in range(2):
+        loads[1 + 2 * c].wait()
+        loads[2 + 2 * c].wait()
         powers = [rhs[c, 0]] + [basis[i, c] for i in range(ITERS)]
         x[c, 0] = sum(s * v for s, v in zip(values[:ITERS], powers))
         r[c, 0] = powers[0] + sum(s * v for s, v in zip(values[ITERS:], powers[1:]))
@@ -515,7 +523,7 @@
             pltpu.VMEM(scalars.shape, f32),
             pltpu.VMEM(rhs.shape, f32),
             pltpu.VMEM(rhs.shape, f32),
-            pltpu.SemaphoreType.DMA((3,)),
+            pltpu.SemaphoreType.DMA((5,)),
             pltpu.SemaphoreType.DMA((4,)),
         ],
         compiler_params=pltpu.CompilerParams(vmem_limit_bytes=63 * 1024 * 1024),

time: 45.6 us -> 45.4 us (level)
  no operation moved by 1% of the time
where the time goes in v7:
time: 45.4 us; the launch traced here: 45.1 us
  Pallas kernels  43.8 us (96%)
  between operations  1.29 us (3%)
    pallas_call x1, Pallas kernels, body(): pl.pallas_call(functools.partial(kernel, ny, nz, nx), out_shape=(jax.Shap...  42 us
    pallas_call x1, Pallas kernels, body(): pl.pallas_call(combine, out_shape=(out, out), in_specs=[hbm] * 3, out_spe...  1.84 us

profile of v7, /device:TPU:1, one launch (start us, length us, event | category | flops | bytes accessed | tf_op | source)
XLA Modules:
  0.0 45.1 jit_solution(4054848972398605290)
XLA Ops:
  1.3 42.0 %shard_map.95 = (f32[3,2,8,2048]{3,2,1,0:T(8,128)}, f32[8,128]{1,0:T(8,128)}) custom-call(f32[2,1,8,2048]{3,2,1,0:T(8,128)} %rhs_hbm.3, f32[1,8,2048]{2,1,0:T(8,128)} %across_hbm.1, f32[1,8,2048]{2,1,0:T(8,128)} %down_hbm.1, f32[1,8,2048]{2,1,0:T(8,128)} %anchor_hbm.1, s32[1,1,1024]{2,1,0:T(1,128)} %source_hbm.1, s32[1,1,1024]{2,1,0:T(1,128)} %target_hbm.1, ...), custom_call_target="tpu_custom_call" | custom-call | tf_op jit(solution)/shard_map/pallas_call | solution.py:472
  43.3 1.8 %shard_map.96 = (f32[2,1,8,2048]{3,2,1,0:T(8,128)}, f32[2,1,8,2048]{3,2,1,0:T(8,128)}) custom-call(f32[2,1,8,2048]{3,2,1,0:T(8,128)} %rhs_hbm.3, f32[3,2,8,2048]{3,2,1,0:T(8,128)} %get-tuple-element.4.basis_hbm, f32[8,128]{1,0:T(8,128)} %get-tuple-element.5.scalars_hbm), custom_call_target="tpu_custom_call" | custom-call | tf_op jit(solution)/shard_map/pallas_call | solution.py:515

commit v8 on v7

--- a/solution.py
+++ b/solution.py
@@ -137,8 +137,7 @@
     hot_source,
     hot_target,
     mask_source,
-    mask_left,
-    mask_right,
+    mask_target,
     basis,
     slot_out,
     rim_out,
@@ -281,29 +280,32 @@
 
     for k in range(ITERS):
         base = 2 + 4 * k
-        own = looked_up(pieces(stacked(field), 2), hot_source, [mask_source], 2)
+        table = pieces(stacked(field), 2)
+        own = looked_up(table, hot_source, [mask_source], 2)
         for c in range(2):
             point_out[k, 0, c : c + 1, :] = own[c]
         own_copy = send(point_out.at[k, 0], point_in.at[k, 0], after, base + 2)
         if k > 0:
             halo = post_halo(field, k)
-        right = [jnp.where(col_id == cols - 1, 0.0, pltpu.roll(f, cols - 1, 1)) for f in field]
         if k == 0:
             copies[0].wait_recv()
-            low, place = split(slot_in[4].astype(jnp.int32))
-            hot_target[...] = (low_id == low).astype(jnp.float32).astype(jnp.bfloat16)
-            for mask, one, two in ((mask_left, 0, 2), (mask_right, 1, 3)):
-                mask[...] = jnp.where(
+            node = slot_in[4].astype(jnp.int32)
+            for side in range(2):
+                low, place = split(node + side)
+                half = slice(side * slots, (side + 1) * slots)
+                hot_target[:, half] = (low_id == low).astype(jnp.float32).astype(jnp.bfloat16)
+                mask_target[:, half] = jnp.where(
                     place_id == place,
-                    slot_in[one],
-                    jnp.where(place_id == place + 1, slot_in[two], 0.0),
+                    slot_in[side],
+                    jnp.where(place_id == place + 1, slot_in[2 + side], 0.0),
                 )
-        table = jnp.concatenate([pieces(stacked(field), 2), pieces(stacked(right), 2)], 0)
-        there = looked_up(table, hot_target, [mask_left, mask_right], 2)
+        both = looked_up(table, hot_target, [mask_target], 2)
+        there = [b[:, :slots] + b[:, slots:] for b in both]
         for c in range(2):
             point_out[k, 1, c : c + 1, :] = there[c]
         there_copy = send(point_out.at[k, 1], point_in.at[k, 1], before, base + 3)
 
+        right = [jnp.where(col_id == cols - 1, 0.0, pltpu.roll(f, cols - 1, 1)) for f in field]
         image, energy = [], None
         for c in range(2):
             f = field[c]
@@ -335,9 +337,8 @@
         def onward():
             own_copy.wait_recv()
             error_in = [there[c] - point_in[k, 0, c : c + 1, :] for c in range(2)]
-            left = unstacked(spread(error_in, mask_left, hot_target, 2), rows, highs)
-            more = unstacked(spread(error_in, mask_right, hot_target, 2), rows, highs)
-            return [a + pltpu.roll(b, 1, 1) for a, b in zip(left, more)]
+            twice = [jnp.concatenate([e, e], 1) for e in error_in]
+            return unstacked(spread(twice, mask_target, hot_target, 2), rows, highs)
 
         if k < ITERS - 1:
             image = [a + b for a, b in zip(image, onward())]
@@ -487,10 +488,9 @@
             pltpu.VMEM(weight.shape, f32),
             pltpu.SMEM(count.shape, jnp.int32),
             pltpu.VMEM((LOW, slots), bf16),
-            pltpu.VMEM((LOW, slots), bf16),
+            pltpu.VMEM((LOW, 2 * slots), bf16),
             pltpu.VMEM((places, slots), f32),
-            pltpu.VMEM((places, slots), f32),
-            pltpu.VMEM((places, slots), f32),
+            pltpu.VMEM((places, 2 * slots), f32),
             pltpu.VMEM((ITERS, 2, rows, cols), f32),
             pltpu.VMEM((5, 1, slots), f32),
             pltpu.VMEM((1, cols), f32),

time: 45.4 us -> 45.7 us (level)
  no operation moved by 1% of the time
where the time goes in v8:
time: 45.7 us; the launch traced here: 45.4 us
  Pallas kernels  44.1 us (96%)
  between operations  1.29 us (3%)
    pallas_call x1, Pallas kernels, body(): pl.pallas_call(functools.partial(kernel, ny, nz, nx), out_shape=(jax.Shap...  42.3 us
    pallas_call x1, Pallas kernels, body(): pl.pallas_call(combine, out_shape=(out, out), in_specs=[hbm] * 3, out_spe...  1.84 us

profile of v8, /device:TPU:1, one launch (start us, length us, event | category | flops | bytes accessed | tf_op | source)
XLA Modules:
  0.0 45.4 jit_solution(7362452049977606934)
XLA Ops:
  1.3 42.3 %shard_map.95 = (f32[3,2,8,2048]{3,2,1,0:T(8,128)}, f32[8,128]{1,0:T(8,128)}) custom-call(f32[2,1,8,2048]{3,2,1,0:T(8,128)} %rhs_hbm.3, f32[1,8,2048]{2,1,0:T(8,128)} %across_hbm.1, f32[1,8,2048]{2,1,0:T(8,128)} %down_hbm.1, f32[1,8,2048]{2,1,0:T(8,128)} %anchor_hbm.1, s32[1,1,1024]{2,1,0:T(1,128)} %source_hbm.1, s32[1,1,1024]{2,1,0:T(1,128)} %target_hbm.1, ...), custom_call_target="tpu_custom_call" | custom-call | tf_op jit(solution)/shard_map/pallas_call | solution.py:473
  43.6 1.8 %shard_map.96 = (f32[2,1,8,2048]{3,2,1,0:T(8,128)}, f32[2,1,8,2048]{3,2,1,0:T(8,128)}) custom-call(f32[2,1,8,2048]{3,2,1,0:T(8,128)} %rhs_hbm.3, f32[3,2,8,2048]{3,2,1,0:T(8,128)} %get-tuple-element.4.basis_hbm, f32[8,128]{1,0:T(8,128)} %get-tuple-element.5.scalars_hbm), custom_call_target="tpu_custom_call" | custom-call | tf_op jit(solution)/shard_map/pallas_call | solution.py:515

commit v9 on v7

--- a/solution.py
+++ b/solution.py
@@ -187,32 +187,32 @@
     far_first = lambda o: -sum(min(d, n - d) for d, n in zip(o, (ny, nz, nx // 2, 2)))
     groups = [peers(sorted(plane, key=far_first)), peers(sorted(line, key=far_first))]
 
-    barrier = pltpu.get_barrier_semaphore()
-    met = [after, before, below, above] + one_hop
-    for peer in met:
-        pl.semaphore_signal(barrier, inc=1, device_id=peer, device_id_type=MESH)
-
-    def greet(stage, who):
-        for peer in who:
-            pl.semaphore_signal(greet_sem.at[stage], inc=1, device_id=peer, device_id_type=MESH)
-
     loads = [
         pltpu.make_async_copy(src, dst, load_sem.at[i])
         for i, (src, dst) in enumerate(
             [
                 (count_hbm, count_ref),
                 (weight_hbm, weight_ref),
+                (target_hbm, target_ref),
                 (source_hbm, source_ref),
                 (rhs_hbm, rhs_ref),
                 (down_hbm, down_ref),
                 (across_hbm, across_ref),
                 (anchor_hbm, anchor_ref),
-                (target_hbm, target_ref),
             ]
         )
     ]
     for load in loads:
         load.start()
+
+    barrier = pltpu.get_barrier_semaphore()
+    met = [after, before, below, above] + one_hop
+    for peer in met:
+        pl.semaphore_signal(barrier, inc=1, device_id=peer, device_id_type=MESH)
+
+    def greet(stage, who):
+        for peer in who:
+            pl.semaphore_signal(greet_sem.at[stage], inc=1, device_id=peer, device_id_type=MESH)
 
     sent, kept = [], []
 
@@ -235,7 +235,7 @@
     live = ((slot < count_ref[0, 0] * BLOCK) & (gz < n_gz - 1)).astype(jnp.float32)
     for k in range(4):
         slot_out[k] = weight_ref[k, 0] * live
-    loads[7].wait()
+    loads[2].wait()
     slot_out[4] = target_ref[0].astype(jnp.float32)
     def post_halo(field, k):
         for c in range(2):
@@ -252,10 +252,10 @@
     ]
     greet(0, one_hop)
 
-    loads[3].wait()
+    loads[4].wait()
     field = [rhs_ref[c, 0] for c in range(2)]
     halo = post_halo(field, 0)
-    loads[4].wait()
+    loads[5].wait()
     rim_out[...] = down_ref[0, rows - 1 :]
     copies.append(send(rim_out, rim_in, below, 1))
 
@@ -266,14 +266,14 @@
         col = node & (cols - 1)
         return col & (LOW - 1), (col >> bits_low) * rows + (node >> bits_cols)
 
-    loads[2].wait()
+    loads[3].wait()
     low, place = split(source_ref[0])
     hot_source[...] = (low_id == low).astype(jnp.float32).astype(jnp.bfloat16)
     mask_source[...] = jnp.where(place_id == place, live, 0.0)
 
 
-    loads[5].wait()
     loads[6].wait()
+    loads[7].wait()
     across, down, anchor = across_ref[0], down_ref[0], anchor_ref[0]
     col_id = lax.broadcasted_iota(jnp.int32, (rows, cols), 1)
     row_id = lax.broadcasted_iota(jnp.int32, (rows, cols), 0)

time: 45.4 us -> 45.4 us (level)
  no operation moved by 1% of the time
where the time goes in v9:
time: 45.4 us; the launch traced here: 45.1 us
  Pallas kernels  43.8 us (96%)
  between operations  1.29 us (3%)
    pallas_call x1, Pallas kernels, body(): pl.pallas_call(functools.partial(kernel, ny, nz, nx), out_shape=(jax.Shap...  42 us
    pallas_call x1, Pallas kernels, body(): pl.pallas_call(combine, out_shape=(out, out), in_specs=[hbm] * 3, out_spe...  1.84 us

profile of v9, /device:TPU:1, one launch (start us, length us, event | category | flops | bytes accessed | tf_op | source)
XLA Modules:
  0.0 45.1 jit_solution(10058986264069914087)
XLA Ops:
  1.3 42.0 %shard_map.95 = (f32[3,2,8,2048]{3,2,1,0:T(8,128)}, f32[8,128]{1,0:T(8,128)}) custom-call(f32[2,1,8,2048]{3,2,1,0:T(8,128)} %rhs_hbm.3, f32[1,8,2048]{2,1,0:T(8,128)} %across_hbm.1, f32[1,8,2048]{2,1,0:T(8,128)} %down_hbm.1, f32[1,8,2048]{2,1,0:T(8,128)} %anchor_hbm.1, s32[1,1,1024]{2,1,0:T(1,128)} %source_hbm.1, s32[1,1,1024]{2,1,0:T(1,128)} %target_hbm.1, ...), custom_call_target="tpu_custom_call" | custom-call | tf_op jit(solution)/shard_map/pallas_call | solution.py:472
  43.3 1.8 %shard_map.96 = (f32[2,1,8,2048]{3,2,1,0:T(8,128)}, f32[2,1,8,2048]{3,2,1,0:T(8,128)}) custom-call(f32[2,1,8,2048]{3,2,1,0:T(8,128)} %rhs_hbm.3, f32[3,2,8,2048]{3,2,1,0:T(8,128)} %get-tuple-element.4.basis_hbm, f32[8,128]{1,0:T(8,128)} %get-tuple-element.5.scalars_hbm), custom_call_target="tpu_custom_call" | custom-call | tf_op jit(solution)/shard_map/pallas_call | solution.py:515
